TPU v7x, 1024 devices: a whole 4x4x32 slice. The times are simulated.
1024 devices in a mesh: dp: 32 (over x, y, core), head: 32 (over z).
Axes of the slice: x: 4, y: 4, z: 32, core: 2. Of those that a mesh axis runs over, the one named last changes fastest.
Arguments:
- text: bfloat16 [4096, 8192], P('dp'), may hold values from -6 to 6
- q_weight: bfloat16 [8192, 4096], P(None, 'head'), may hold values from -0.0625 to 0.0625
- q_gain: float32 [128], replicated, may hold values from 0.1 to 1.9
- enc_hidden: bfloat16 [8192, 1280], P(('dp', 'head')), may hold values from -100 to 100
- enc_branch: bfloat16 [8192, 1280], P(('dp', 'head')), may hold values from -6 to 6
- enc_gate: float32 [1], replicated, may hold values from 0.3 to 1.5
- enc_gain: float32 [1280], replicated, may hold values from 0.1 to 1.9
- enc_bias: float32 [1280], replicated, may hold values from -3 to 3
- proj_weight: bfloat16 [1280, 8192], P(None, 'head'), may hold values from -0.15625 to 0.15625
- proj_bias: float32 [8192], P('head'), may hold values from -3 to 3
- kv_weight: bfloat16 [8192, 1024], P('head'), may hold values from -0.0625 to 0.0625
- k_gain: float32 [128], replicated, may hold values from 0.1 to 1.9
- attn_gate: float32 [1], replicated, may hold values from 0.3 to 1.5
- o_weight: bfloat16 [4096, 8192], P(None, 'head'), may hold values from -0.09375 to 0.09375
- d_update: bfloat16 [4096, 8192], P('dp', 'head'), may hold values from -12 to 12
- tile_counts: int32 [32, 3], P('dp'), may hold values from 1 to 4, 8 in all within a row
- image_sample: int32 [32, 3], P('dp'), may hold values from 0 to 1, as said below
- text_lengths: int32 [32, 2], P('dp'), may hold values from 1 to 64, as said below
Outputs:
- attn: bfloat16 [4096, 4096], P('dp', 'head')
- d_text: bfloat16 [4096, 8192], P('dp', 'head')
- d_features: bfloat16 [8192, 1280], P(('dp', 'head'))
- d_q_gain: float32 [128], replicated
- d_k_gain: float32 [128], replicated
Inputs may be any that keep to these rules, and one draw needn't show every extreme that they name: `image_sample`: every sample of a group has at least one image. `text_lengths`: in every group one sample uses all 64 slots.
All inputs are finite; a program needn't handle non-finite values.
Results may differ from a plain program's by a relative error of at most 0.034.
Values may be sent and summed in bfloat16 or wider, within the bound.
A program may use at most 32 MiB of HBM per device.

v0:
```python
import jax
import jax.numpy as jnp
from jax import lax
from jax.sharding import PartitionSpec as P

TXT = 64
TILE = 32


EPSILON = 1e-05


def key_samples(tiles, owners, count):
    ends = jnp.cumsum(tiles, dtype=jnp.int32) * TILE
    key_rows = jnp.arange(count, dtype=jnp.int32)
    image_index = jnp.sum(
        (key_rows[:, None] >= ends[None, :]).astype(jnp.int32), axis=1, dtype=jnp.int32
    )
    picked = image_index[:, None] == jnp.arange(tiles.shape[0], dtype=jnp.int32)[None, :]
    return jnp.sum(jnp.where(picked, owners[None, :], 0), axis=1, dtype=jnp.int32)


def slot_masks(lengths, count, key_sample):
    slots = jnp.arange(count, dtype=jnp.int32)
    sample = slots // TXT
    chosen = sample[:, None] == jnp.arange(lengths.shape[0], dtype=jnp.int32)[None, :]
    limit = jnp.sum(jnp.where(chosen, lengths[None, :], 0), axis=1, dtype=jnp.int32)
    valid = (slots % TXT < limit).astype(jnp.float32)
    allowed = (sample[:, None] == key_sample[None, :]).astype(jnp.float32)
    return (allowed, valid)


def on_device(
    text,
    q_weight,
    q_gain,
    enc_hidden,
    enc_branch,
    enc_gate,
    enc_gain,
    enc_bias,
    proj_weight,
    proj_bias,
    kv_weight,
    k_gain,
    attn_gate,
    o_weight,
    d_update,
    tile_counts,
    image_sample,
    text_lengths,
):
    width = q_gain.shape[0]
    kv_heads = kv_weight.shape[1] // (2 * width)
    n_heads = lax.axis_size("head")
    head_pos = lax.axis_index("head")
    sharing = n_heads // kv_heads
    own_kv = head_pos // sharing
    scale = width ** (-0.5)
    enc_rows = enc_hidden.shape[0]
    slot_count = text.shape[0]
    features = enc_hidden.astype(jnp.float32) + jnp.tanh(enc_gate[0]) * enc_branch.astype(
        jnp.float32
    )
    centered = features - jnp.mean(features, axis=1, keepdims=True)
    inv_std = lax.rsqrt(jnp.mean(centered * centered, axis=1, keepdims=True) + EPSILON)
    unit_feat = centered * inv_std
    normed = (unit_feat * enc_gain + enc_bias).astype(jnp.bfloat16)
    proj_feat = (
        jnp.dot(
            lax.all_gather(normed, "head", axis=0, tiled=True),
            proj_weight,
            preferred_element_type=jnp.float32,
        )
        + proj_bias
    ).astype(jnp.bfloat16)
    group_rows = proj_feat.shape[0]
    total = lax.psum(jnp.dot(proj_feat, kv_weight, preferred_element_type=jnp.float32), "head")
    owned = lax.dynamic_slice_in_dim(total, head_pos * enc_rows, enc_rows, 0)
    every = total.reshape(group_rows, kv_heads, 2 * width)
    own_block = lax.dynamic_slice_in_dim(every, own_kv, 1, 1)[:, 0]
    own_keys = own_block[:, :width]
    own_unit = own_keys * lax.rsqrt(jnp.mean(own_keys * own_keys, axis=1, keepdims=True) + EPSILON)
    kv_rows = jnp.concatenate([own_unit * k_gain, own_block[:, width:]], axis=1).astype(
        jnp.bfloat16
    )
    owner_kv = owned.reshape(enc_rows, kv_heads, 2 * width)
    key_pre = owner_kv[:, :, :width]
    inv_key = lax.rsqrt(jnp.mean(key_pre * key_pre, axis=2, keepdims=True) + EPSILON)
    key_unit = key_pre * inv_key
    query_pre = jnp.dot(text, q_weight, preferred_element_type=jnp.float32)
    inv_query = lax.rsqrt(jnp.mean(query_pre * query_pre, axis=1, keepdims=True) + EPSILON)
    query_unit = query_pre * inv_query
    q_scaled = (query_unit * q_gain * scale).astype(jnp.bfloat16)
    key_sample = key_samples(tile_counts[0], image_sample[0], kv_rows.shape[0])
    allowed, valid = slot_masks(text_lengths[0], slot_count, key_sample)
    keys = kv_rows[:, :width]
    values = kv_rows[:, width:]
    scores = jnp.einsum("td,rd->tr", q_scaled, keys, preferred_element_type=jnp.float32)
    weighted = jnp.exp(scores) * allowed
    probs = weighted / jnp.sum(weighted, axis=1, keepdims=True)
    probs_low = probs.astype(jnp.bfloat16)
    attn = (jnp.dot(probs_low, values, preferred_element_type=jnp.float32) * valid[:, None]).astype(
        jnp.bfloat16
    )
    partial_terms = jnp.einsum("tf,cf->tc", d_update, o_weight, preferred_element_type=jnp.float32)
    attn_total = lax.psum_scatter(partial_terms, "head", scatter_dimension=1, tiled=True)
    d_attn = (jnp.tanh(attn_gate[0]) * attn_total * valid[:, None]).astype(jnp.bfloat16)
    d_probs = jnp.einsum("td,rd->tr", d_attn, values, preferred_element_type=jnp.float32)
    delta = jnp.sum(d_probs * probs, axis=1, keepdims=True)
    d_scores = (probs * (d_probs - delta)).astype(jnp.bfloat16)
    d_q_scaled = jnp.dot(d_scores, keys, preferred_element_type=jnp.float32)
    d_keys = jnp.einsum("tr,td->rd", d_scores, q_scaled, preferred_element_type=jnp.float32).astype(
        jnp.bfloat16
    )
    d_values = jnp.einsum(
        "tr,td->rd", probs_low, d_attn, preferred_element_type=jnp.float32
    ).astype(jnp.bfloat16)
    kv_grads = jnp.concatenate([d_keys, d_values], axis=1)
    returned = lax.all_to_all(kv_grads, "head", split_axis=0, concat_axis=1, tiled=True)
    kv_sum = (
        returned.reshape(enc_rows, kv_heads, sharing, 2 * width).astype(jnp.float32).sum(axis=2)
    )
    query_grad = d_q_scaled * q_gain * scale
    d_queries = (
        inv_query
        * (query_grad - query_unit * jnp.mean(query_grad * query_unit, axis=1, keepdims=True))
    ).astype(jnp.bfloat16)
    text_terms = jnp.einsum("td,fd->tf", d_queries, q_weight, preferred_element_type=jnp.float32)
    d_text = lax.psum_scatter(
        text_terms.astype(jnp.bfloat16), "head", scatter_dimension=1, tiled=True
    )
    d_key_part = kv_sum[:, :, :width]
    key_grad = d_key_part * k_gain
    d_key_pre = inv_key * (
        key_grad - key_unit * jnp.mean(key_grad * key_unit, axis=2, keepdims=True)
    )
    d_projected = (
        jnp.concatenate([d_key_pre, kv_sum[:, :, width:]], axis=2)
        .reshape(enc_rows, kv_heads * 2 * width)
        .astype(jnp.bfloat16)
    )
    d_proj_feat = jnp.einsum(
        "rc,dc->rd",
        lax.all_gather(d_projected, "head", axis=0, tiled=True),
        kv_weight,
        preferred_element_type=jnp.float32,
    ).astype(jnp.bfloat16)
    d_normed = lax.psum_scatter(
        jnp.einsum("rd,ed->re", d_proj_feat, proj_weight, preferred_element_type=jnp.float32),
        "head",
        scatter_dimension=0,
        tiled=True,
    )
    feat_grad = d_normed * enc_gain
    d_features = inv_std * (
        feat_grad
        - jnp.mean(feat_grad, axis=1, keepdims=True)
        - unit_feat * jnp.mean(feat_grad * unit_feat, axis=1, keepdims=True)
    )
    query_part = jnp.sum(d_q_scaled * query_unit, axis=0) * scale
    key_part = jnp.sum(d_key_part * key_unit, axis=(0, 1))
    d_q_gain, d_k_gain = lax.psum((query_part, key_part), ("dp", "head"))
    return (attn, d_text, d_features.astype(jnp.bfloat16), d_q_gain, d_k_gain)


def solution(mesh):
    in_specs = (
        P("dp", None),
        P(None, "head"),
        P(),
        P(("dp", "head"), None),
        P(("dp", "head"), None),
        P(),
        P(),
        P(),
        P(None, "head"),
        P("head"),
        P("head", None),
        P(),
        P(),
        P(None, "head"),
        P("dp", "head"),
        P("dp", None),
        P("dp", None),
        P("dp", None),
    )
    out_specs = (P("dp", "head"), P("dp", "head"), P(("dp", "head"), None), P(), P())
    return jax.shard_map(
        on_device, mesh=mesh, in_specs=in_specs, out_specs=out_specs, check_vma=False
    )
```

profile of v0, /device:TPU:6, one launch (start us, length us, event | category | flops | bytes accessed | tf_op | source)
XLA Modules:
  0.0 845.2 jit_solution(16121028530372677828)
XLA Ops:
  7.2 0.0 copy-start
  7.2 0.0 all-reduce.3.cloned.1.call-start
  8.1 0.9 fusion.13
  8.9 0.9 multiply_reduce_fusion.6
  9.9 0.8 add_convert_fusion
  10.7 71.5 %all_gather.6 = bf16[256,1280]{1,0:T(8,128)(2,1)S(1)} all-gather(bf16[8,1280]{1,0:T(8,128)(2,1)S(1)} %add_convert_fusion), channel_id=1, replica_groups=mesh['dp'=32,'head'=32] {'head'}, dimensions={0}, use_global_device_ids=true | all-gather | bytes 675840 | tf_op jit(solution)/shard_map/all_gather | solution.py:71
  82.2 3.0 fusion.1
  85.3 0.0 all-reduce.3.cloned.1.call-update
  85.3 0.0 reduce-scatter.4.cloned.1.call-start
  85.4 3.8 fusion.18
  89.1 0.0 reduce-scatter.4.cloned.1.call-update
  89.9 0.2 reduce-window.8
  90.1 0.1 convert_reduce_fusion
  90.2 0.1 fusion.14
  90.2 0.1 select_reduce_fusion
  90.3 2.5 multiply_reduce_fusion.4
  92.9 0.0 copy-start.8
  92.9 250.5 %all-reduce.3.cloned.1.call-done = f32[256,1024]{1,0:T(8,128)} async-done(((f32[256,1024]{1,0:T(8,128)}), f32[256,1024]{1,0:T(8,128)}) %all-reduce.3.cloned.1.call-update) | async-done | bytes 1048592 | tf_op jit(solution)/shard_map/psum | solution.py:78
  343.5 1.7 reshape.143
  345.2 0.2 constant_dynamic-slice_fusion
  345.5 0.1 multiply_reduce_fusion.1
  345.6 0.4 fusion.17
  346.0 129.4 %reduce-scatter.4.cloned.1.call-done = f32[128,128]{1,0:T(8,128)} async-done(((f32[128,4096]{1,0:T(8,128)}), f32[128,128]{1,0:T(8,128)}) %reduce-scatter.4.cloned.1.call-update) | async-done | bytes 65552 | tf_op jit(solution)/shard_map/reduce_scatter | solution.py:107
  475.5 1.1 multiply_reduce_fusion
  476.6 0.1 multiply_convert_fusion
  476.7 0.2 convolution_convert_fusion.2
  477.0 1.1 convolution_convert_fusion.3
  478.1 0.8 copy.29
  478.9 17.1 %all-to-all-start = ((bf16[32,8,256]{2,1,0:T(8,128)(2,1)}), bf16[32,8,256]{2,1,0:T(8,128)(2,1)S(1)}, u32[]{:S(2)}, u32[]{:S(2)}) async-start(bf16[32,8,256]{2,1,0:T(8,128)(2,1)} %bitcast.7), calls=%async_computation.2 | async-start | bytes 262144 | tf_op jit(solution)/shard_map/all_to_all | solution.py:120
  495.9 0.0 reduce-scatter.8.cloned.1.call-start
  496.0 0.8 constant_dynamic-slice_fusion.1
  496.8 0.1 multiply_reduce_fusion.10
  496.9 26.6 %all-to-all-done = bf16[32,8,256]{2,1,0:T(8,128)(2,1)S(1)} async-done(((bf16[32,8,256]{2,1,0:T(8,128)(2,1)}), bf16[32,8,256]{2,1,0:T(8,128)(2,1)S(1)}, u32[]{:S(2)}, u32[]{:S(2)}) %all-to-all-start) | async-done | bytes 131104 | tf_op jit(solution)/shard_map/all_to_all | solution.py:120
  523.5 0.6 multiply_reduce_fusion.8
  524.1 0.1 multiply_convert_fusion.7
  524.2 54.5 %all_gather.7 = bf16[256,1024]{1,0:T(8,128)(2,1)S(1)} all-gather(bf16[8,1024]{1,0:T(8,128)(2,1)S(1)} %bitcast.38), channel_id=1, replica_groups=mesh['dp'=32,'head'=32] {'head'}, dimensions={0}, use_global_device_ids=true | all-gather | bytes 540672 | tf_op jit(solution)/shard_map/all_gather | solution.py:145
  578.7 2.9 fusion.2
  581.7 0.0 reduce-scatter.8.cloned.1.call-update
  581.7 0.0 reduce-scatter.6.cloned.1.call-start
  581.7 1.3 multiply_reduce_fusion.2
  583.0 2.8 convolution_convert_fusion
  585.9 0.0 reduce-scatter.6.cloned.1.call-update
  585.9 0.9 copy-done.3
  586.8 0.8 fusion.4
  587.7 152.1 %all-reduce = (f32[128]{0:T(128)}, f32[128]{0:T(128)}) all-reduce(f32[128]{0:T(128)S(1)} %broadcast_multiply_fusion.1, f32[128]{0:T(128)S(1)} %copy-done.14), channel_id=1, replica_groups=mesh['dp'=32,'head'=32] {'dp','head'}, use_global_device_ids=true, to_apply=%region_21.22 | all-reduce | flops 256 | bytes 2048 | tf_op jit(solution)/shard_map/psum | solution.py:163
  739.7 1.0 multiply_reduce_fusion.7
  740.7 1.5 multiply_convert_fusion.5
  742.2 96.5 %reduce-scatter.6.cloned.1.call-done = bf16[128,256]{1,0:T(8,128)(2,1)} async-done(((bf16[128,8192]{1,0:T(8,128)(2,1)}), bf16[128,256]{1,0:T(8,128)(2,1)}) %reduce-scatter.6.cloned.1.call-update) | async-done | bytes 65552 | tf_op jit(solution)/shard_map/reduce_scatter | solution.py:130
  (55 shorter events, 0.2 us)
Async XLA Ops:
  7.2 83.2 %copy-start = (bf16[8192,128]{1,0:T(8,128)(2,1)S(1)}, bf16[8192,128]{1,0:T(8,128)(2,1)}, u32[]{:S(2)}) copy-start(bf16[8192,128]{1,0:T(8,128)(2,1)} %param.19) | copy-start | bytes 6291460
  7.2 336.3 %all-reduce.3.cloned.1.call-start = ((), (), s32[]{:S(2)}) async-start(), calls=%async_computation.4 | async-start | bytes 2097152 | tf_op jit(solution)/shard_map/psum | solution.py:78
  82.2 3.1 copy-start.7
  85.3 390.1 %reduce-scatter.4.cloned.1.call-start = ((), (), s32[]{:S(2)}) async-start(), calls=%async_computation.5 | async-start | bytes 2162688 | tf_op jit(solution)/shard_map/reduce_scatter | solution.py:107
  89.1 0.7 copy-start.16
  89.1 1.0 copy-start.17
  89.1 1.1 copy-start.15
  90.3 385.1 %copy-start.18 = (f32[128]{0:T(128)}, f32[128]{0:T(128)S(1)}, u32[]{:S(2)}) copy-start(f32[128]{0:T(128)S(1)} %compare_convert_fusion) | copy-start | bytes 1540
  92.9 252.7 %copy-start.8 = (f32[128]{0:T(128)S(1)}, f32[128]{0:T(128)}, u32[]{:S(2)}) copy-start(f32[128]{0:T(128)} %param.29) | copy-start | bytes 1540
  92.9 252.7 %copy-start.9 = (f32[128]{0:T(128)S(1)}, f32[128]{0:T(128)}, u32[]{:S(2)}) copy-start(f32[128]{0:T(128)} %param.20) | copy-start | bytes 1540
  92.9 383.8 %copy-start.10 = (f32[128]{0:T(128)}, f32[128]{0:T(128)S(1)}, u32[]{:S(2)}) copy-start(f32[128]{0:T(128)S(1)} %add_rsqrt_fusion.3) | copy-start | bytes 1540
  345.4 233.3 %copy-start.1 = (bf16[1280,256]{1,0:T(8,128)(2,1)S(1)}, bf16[1280,256]{1,0:T(8,128)(2,1)}, u32[]{:S(2)}) copy-start(bf16[1280,256]{1,0:T(8,128)(2,1)} %param.26) | copy-start | bytes 1966084
  345.4 178.7 %copy-start.2 = (f32[256,1,256]{2,0,1:T(8,128)}, f32[256,1,256]{2,0,1:T(8,128)S(1)}, u32[]{:S(2)}) copy-start(f32[256,1,256]{2,0,1:T(8,128)S(1)} %copy.34) | copy-start | bytes 786436
  345.6 131.1 %copy-start.11 = (f32[256]{0:T(256)}, f32[256]{0:T(256)S(1)}, u32[]{:S(2)}) copy-start(f32[256]{0:T(256)S(1)} %add_rsqrt_fusion.1) | copy-start | bytes 3076
  346.0 130.7 %copy-start.12 = (f32[128]{0:T(128)}, f32[128]{0:T(128)S(1)}, u32[]{:S(2)}) copy-start(f32[128]{0:T(128)S(1)} %get-tuple-element.15) | copy-start | bytes 1540
  478.9 44.6 %all-to-all-start = ((bf16[32,8,256]{2,1,0:T(8,128)(2,1)}), bf16[32,8,256]{2,1,0:T(8,128)(2,1)S(1)}, u32[]{:S(2)}, u32[]{:S(2)}) async-start(bf16[32,8,256]{2,1,0:T(8,128)(2,1)} %bitcast.7), calls=%async_computation.2 | async-start | bytes 262144 | tf_op jit(solution)/shard_map/all_to_all | solution.py:120
  495.9 243.8 %reduce-scatter.8.cloned.1.call-start = ((), (), s32[]{:S(2)}) async-start(), calls=%async_computation.7 | async-start | bytes 1351680 | tf_op jit(solution)/shard_map/reduce_scatter | solution.py:149
  581.7 257.0 %reduce-scatter.6.cloned.1.call-start = ((), (), s32[]{:S(2)}) async-start(), calls=%async_computation.6 | async-start | bytes 2162688 | tf_op jit(solution)/shard_map/reduce_scatter | solution.py:130
  585.9 0.9 copy-start.3
  585.9 1.0 copy-start.13
  585.9 1.0 copy-start.19
  585.9 1.8 copy-start.14
  585.9 153.8 %copy-start.4 = (bf16[8,1280]{1,0:T(8,128)(2,1)S(1)}, bf16[8,1280]{1,0:T(8,128)(2,1)}, u32[]{:S(2)}) copy-start(bf16[8,1280]{1,0:T(8,128)(2,1)} %param.22) | copy-start | bytes 61444
  585.9 153.8 %copy-start.5 = (bf16[8,1280]{1,0:T(8,128)(2,1)S(1)}, bf16[8,1280]{1,0:T(8,128)(2,1)}, u32[]{:S(2)}) copy-start(bf16[8,1280]{1,0:T(8,128)(2,1)} %param.21) | copy-start | bytes 61444
  585.9 153.8 %copy-start.6 = (f32[1280]{0:T(1024)S(1)}, f32[1280]{0:T(1024)}, u32[]{:S(2)}) copy-start(f32[1280]{0:T(1024)} %param.24) | copy-start | bytes 15364
Sparse Core Ops, SparseCore 0:
  85.4 257.9 all-reduce.2
  347.2 128.1 reduce-scatter.3
  581.8 120.2 reduce-scatter.7
  706.3 132.2 reduce-scatter.5
where the time goes:
time: 846 us; the launch traced here: 845 us
  waiting for transfers between devices  503 us (59%)
  blocking collectives  278 us (33%)
  matrix products  20.1 us (2%)
  starting transfers between devices  17.2 us (2%)
  between operations  15.6 us (2%)
    psum x1, waiting for transfers between devices, on_device(): lax.psum(jnp.dot(proj_feat, kv_weight, preferred_element_type=jnp.float32...  251 us
    psum x1, blocking collectives, on_device(): d_q_gain, d_k_gain = lax.psum((query_part, key_part), ('dp', 'head'))  152 us
    reduce_scatter x1, waiting for transfers between devices, on_device(): lax.psum_scatter(partial_terms, 'head', scatter_dimension=1, tiled=True)  129 us
    reduce_scatter x1, waiting for transfers between devices, on_device(): lax.psum_scatter(text_terms.astype(jnp.bfloat16), 'head', scatter_dimensi...  96.5 us
    all_gather x1, blocking collectives, on_device(): lax.all_gather(normed, 'head', axis=0, tiled=True)  71.5 us
    all_gather x1, blocking collectives, on_device(): lax.all_gather(d_projected, 'head', axis=0, tiled=True)  54.5 us
    all_to_all x1, waiting for transfers between devices, on_device(): lax.all_to_all(kv_grads, 'head', split_axis=0, concat_axis=1, tiled=True)  26.6 us
    all_to_all x1, starting transfers between devices, on_device(): lax.all_to_all(kv_grads, 'head', split_axis=0, concat_axis=1, tiled=True)  17.1 us
  transfers between devices with their start and end apart: 5, of which 4 were waited for; matrix products, arithmetic and copies ran while one was open for 2% of the time, Pallas kernels for 0%

commit v1 on v0

v1 whole, which is shorter than its diff:
```python
import jax
import jax.numpy as jnp
from jax import lax
from jax.experimental import pallas as pl
from jax.experimental.pallas import tpu as pltpu
from jax.sharding import PartitionSpec as P

N = 32
TXT = 64
TILE = 32
W = 128
ENC = 1280
HALF = 640
AUG = 1408
TILES = 22
EPSILON = 1e-05
MESH = pl.DeviceIdType.MESH
F32 = jnp.float32
BF16 = jnp.bfloat16

S_NRM, S_WRS, S_WAG, S_PLA, S_KV, S_KVG, S_DPA, S_FR, S_G1, S_G2, S_QT1, S_QT2, S_DQ = range(13)


def nn(a, b):
    return lax.dot_general(a, b, (((1,), (0,)), ((), ())), preferred_element_type=F32)


def nt(a, b):
    return lax.dot_general(a, b, (((1,), (1,)), ((), ())), preferred_element_type=F32)


def tn(a, b):
    return lax.dot_general(a, b, (((0,), (0,)), ((), ())), preferred_element_type=F32)


def kernel(
    tiles, owners, lengths, enc_gate, attn_gate,
    q_gain, k_gain, enc_hidden, enc_branch, enc_gain, enc_bias, proj_bias, d_update,
    text, q_weight, proj_weight, kv_weight, o_weight,
    attn_out, text_out, feat_out, qg_out, kg_out,
    text_v, qw_v, pw_v, kvw_v, ow_v,
    nrm, wt, wr, ws, wf, pp, pr, kvs, kvr, kgs, kgr, dps, dpr, fs, fr,
    gs, gr, gs2, gr2, c_right, c_left, dqa, qt,
    qu_v, qs_v, qi_v, ku_v, ki_v, unit_v, istd_v, acc,
    load_sem, send, recv, ring_send, ring_recv, dq_recv,
):
    dp = lax.axis_index("dp")
    z = lax.axis_index("head")

    def z_at(k):
        return lax.rem(z + k + 2 * N, N)

    def remote(src, dst, s_sem, r_sem, dev):
        return pltpu.make_async_remote_copy(
            src_ref=src, dst_ref=dst, send_sem=s_sem, recv_sem=r_sem,
            device_id=dev, device_id_type=MESH,
        )

    def wait_for(sem, ref):
        pltpu.make_async_copy(ref, ref, sem).wait()

    def far_first(n):
        step = (n + 1) // 2
        return jnp.where(lax.rem(n, 2) == 1, 16 + step, 16 - step)

    def to_z(stage, src_of, dst):
        def one(n, _):
            to = z_at(far_first(n))
            remote(src_of(to), dst, send.at[stage], recv.at[stage], (dp, to)).start()
            return 0
        lax.fori_loop(0, N - 1, one, 0)

    def to_plane(stage, src_of, dst):
        def one(n, _):
            to = lax.rem(dp + far_first(n), N)
            remote(src_of(to), dst, send.at[stage], recv.at[stage], (to, z)).start()
            return 0
        lax.fori_loop(0, N - 1, one, 0)

    loads = [
        pltpu.make_async_copy(src, dst, load_sem.at[n])
        for n, (src, dst) in enumerate((
            (proj_weight, pw_v), (kv_weight, kvw_v), (o_weight, ow_v),
            (q_weight, qw_v), (text, text_v),
        ))
    ]
    for load in loads:
        load.start()
    wf[...] = jnp.zeros_like(wf)

    barrier = pltpu.get_barrier_semaphore()

    def greet(k, _):
        pl.semaphore_signal(barrier, inc=1, device_id=(dp, z_at(k)), device_id_type=MESH)
        pl.semaphore_signal(
            barrier, inc=1, device_id=(lax.rem(dp + k, N), z), device_id_type=MESH
        )
        return 0

    lax.fori_loop(1, N, greet, 0)

    gate = jnp.tanh(jnp.full((8, ENC), enc_gate[0, 0], F32))
    features = enc_hidden[...].astype(F32) + gate * enc_branch[...].astype(F32)
    centered = features - jnp.mean(features, axis=1, keepdims=True)
    inv_std = lax.rsqrt(jnp.mean(centered * centered, axis=1, keepdims=True) + EPSILON)
    unit = centered * inv_std
    unit_v[...] = unit
    istd_v[...] = jnp.broadcast_to(inv_std, (8, W))
    normed = unit * enc_gain[...] + enc_bias[...]
    nrm[dp] = jnp.concatenate([normed[:, :HALF], normed[:, HALF:]], axis=0).astype(BF16)

    block = dp // 4
    quarter = lax.rem(dp, 4)
    rows0 = 32 * quarter
    loads[0].wait()
    loads[1].wait()
    kv_t = kvw_v[:, pl.ds(pl.multiple_of(W * block, W), W)].astype(F32).T.astype(BF16)
    wt[:, :ENC] = nt(kv_t, pw_v[...]).astype(BF16)
    first_row = lax.broadcasted_iota(jnp.int32, (W, 256), 0) == 0
    bias_rows = jnp.where(first_row, jnp.broadcast_to(proj_bias[...], (W, 256)), 0.0).astype(BF16)
    wt[:, ENC:] = nt(kv_t, bias_rows).astype(BF16)

    def tile_of(ref, t):
        row = pl.multiple_of(rows0 + 16 * (t // 11), 16)
        col = pl.multiple_of(W * lax.rem(t, 11), W)
        return ref.at[pl.ds(row, 16), pl.ds(col, W)]

    own_tile = (11 * z + 15) // 16
    owning = jnp.logical_and(own_tile < TILES, (16 * own_tile) // 11 == z)

    def term(d):
        return nt(d_update[...], ow_v[pl.ds(pl.multiple_of(W * d, W), W), :])

    loads[2].wait()
    c_right[0] = term(z_at(16)).astype(BF16)
    c_left[0] = term(z_at(-15)).astype(BF16)

    pl.semaphore_wait(barrier, 2 * (N - 1))

    def send_tile(n, _):
        t = lax.rem((11 * z_at(16) + 15) // 16 + n, TILES)
        to = (16 * t) // 11

        @pl.when(to != z)
        def _():
            remote(tile_of(wt, t), wr.at[z], send.at[S_WRS], recv.at[S_WRS], (dp, to)).start()
        return 0

    lax.fori_loop(0, TILES, send_tile, 0)

    def ring_copies(s):
        return (
            remote(c_right.at[s], c_right.at[s + 1], ring_send.at[0, s], ring_recv.at[0, s],
                   (dp, z_at(1))),
            remote(c_left.at[s], c_left.at[s + 1], ring_send.at[1, s], ring_recv.at[1, s],
                   (dp, z_at(-1))),
        )

    for copy in ring_copies(0):
        copy.start()
    to_plane(S_NRM, lambda to: nrm.at[dp], nrm.at[dp])

    def ring_steps(low, high):
        def one(s, _):
            own_right = term(z_at(16 - s))
            own_left = term(z_at(s - 15))
            before = ring_copies(s - 1)
            now = ring_copies(s)
            before[0].wait_recv()
            c_right[s] = (c_right[s].astype(F32) + own_right).astype(BF16)
            now[0].start()
            before[1].wait_recv()
            c_left[s] = (c_left[s].astype(F32) + own_left).astype(BF16)
            now[1].start()
            return 0
        lax.fori_loop(low, high, one, 0)

    loads[3].wait()
    loads[4].wait()
    query_pre = nn(text_v[...], qw_v[...])
    inv_query = lax.rsqrt(jnp.mean(query_pre * query_pre, axis=1, keepdims=True) + EPSILON)
    scale = W ** (-0.5)
    query_unit = query_pre * inv_query
    qu_v[...] = query_unit
    qi_v[...] = jnp.broadcast_to(inv_query, (W, W))
    qs_v[...] = (query_unit * q_gain[...] * scale).astype(BF16)

    ring_steps(1, 4)

    @pl.when(owning)
    def _():
        wait_for(recv.at[S_WRS], wr.at[pl.ds(0, N - 1)])
        wr[z] = tile_of(wt, own_tile)[...]
        tile = jnp.sum(wr[...].astype(F32), axis=0).astype(BF16)
        ws[...] = tile
        tile_of(wf, own_tile)[...] = tile
        to_z(S_WAG, lambda to: ws, tile_of(wf, own_tile))

    ring_steps(4, 8)

    @pl.when(owning)
    def _():
        wait_for(recv.at[S_WAG], wr.at[pl.ds(0, TILES - 1)])

    @pl.when(jnp.logical_not(owning))
    def _():
        wait_for(recv.at[S_WAG], wr.at[pl.ds(0, TILES)])

    wait_for(recv.at[S_NRM], nrm.at[pl.ds(0, N - 1)])

    plane = nrm[...].reshape(2 * 256, HALF)
    half_a = nt(plane, wf[:, :HALF]).reshape(N, 16, W)
    half_b = nt(plane, wf[:, HALF:ENC]).reshape(N, 16, W)
    ones = jnp.where(lax.broadcasted_iota(jnp.int32, (8, W), 1) == 0, 1.0, 0.0).astype(BF16)
    bias = nt(ones, wf[:, ENC:])
    pp[...] = half_a[:, :8] + half_b[:, 8:] + bias[None]
    to_plane(S_PLA, lambda to: pp.at[to], pr.at[dp])
    pr[dp] = pp[dp]

    chip = dp // 2
    core = lax.rem(dp, 2)
    part = pl.ds(pl.multiple_of(16 * chip, 16), 16)
    even = lax.rem(z, 2) == core

    @pl.when(even)
    def _():
        to_z(
            S_QT1,
            lambda to: qw_v.at[pl.ds(pl.multiple_of(256 * to + 16 * chip, 16), 16)],
            qt.at[core, z // 2, part],
        )
        qt[core, z // 2, part] = qw_v[pl.ds(pl.multiple_of(256 * z + 16 * chip, 16), 16)]

    ring_steps(8, 10)

    wait_for(recv.at[S_PLA], pr.at[pl.ds(0, N - 1)])
    blocks = jnp.sum(pr[...].reshape(8, 4, 8, W), axis=1)
    for k in range(4):
        key_pre = blocks[2 * k]
        inv_key = lax.rsqrt(jnp.mean(key_pre * key_pre, axis=1, keepdims=True) + EPSILON)
        key_unit = key_pre * inv_key
        ku_v[k] = key_unit
        ki_v[k] = jnp.broadcast_to(inv_key, (8, W))
        kvs[k] = jnp.concatenate([key_unit * k_gain[...], blocks[2 * k + 1]], axis=0).astype(BF16)
    to_z(S_KV, lambda to: kvs.at[to // 8], kvr.at[z])
    kvr[z] = kvs[z // 8]

    ring_steps(10, 13)

    @pl.when(even)
    def _():
        wait_for(recv.at[S_QT1], kvr.at[pl.ds(0, 15)])

    @pl.when(jnp.logical_not(even))
    def _():
        wait_for(recv.at[S_QT1], kvr.at[pl.ds(0, 16)])

    to_plane(S_QT2, lambda to: qt.at[core, :, part], qt.at[core, :, part])

    ring_steps(13, 15)
    own_right = term(z_at(1))
    before = ring_copies(14)
    before[0].wait_recv()
    c_right[15] = (c_right[15].astype(F32) + own_right).astype(BF16)
    last = ring_copies(15)[0]
    last.start()

    wait_for(recv.at[S_KV], kvr.at[pl.ds(0, N - 1)])
    kv_f = kvr[...].astype(F32)
    keys = kv_f[:, :8].reshape(256, W).astype(BF16)
    values = kv_f[:, 8:].reshape(256, W).astype(BF16)
    row = lax.broadcasted_iota(jnp.int32, (W, 256), 1)
    slot = lax.broadcasted_iota(jnp.int32, (W, 256), 0)
    end0 = tiles[0, 0] * TILE
    end1 = end0 + tiles[0, 1] * TILE
    key_sample = jnp.where(
        row < end0, owners[0, 0], jnp.where(row < end1, owners[0, 1], owners[0, 2])
    )
    allowed = jnp.where((slot >= TXT).astype(jnp.int32) == key_sample, 1.0, 0.0)
    slot_w = lax.broadcasted_iota(jnp.int32, (W, W), 0)
    limit = jnp.where(slot_w >= TXT, lengths[0, 1] + TXT, lengths[0, 0])
    valid = jnp.where(slot_w < limit, 1.0, 0.0)
    q_scaled = qs_v[...]
    weighted = jnp.exp(nt(q_scaled, keys)) * allowed
    probs = weighted / jnp.sum(weighted, axis=1, keepdims=True)
    probs_low = probs.astype(BF16)
    attn_out[...] = (nn(probs_low, values) * valid).astype(BF16)

    before[1].wait_recv()
    own = term(z) + c_left[15].astype(F32)
    last.wait_recv()
    attn_total = c_right[16].astype(F32) + own
    d_gate = jnp.tanh(jnp.full((W, W), attn_gate[0, 0], F32))
    d_attn = (d_gate * attn_total * valid).astype(BF16)
    d_probs = nt(d_attn, values)
    delta = jnp.sum(d_probs * probs, axis=1, keepdims=True)
    d_scores_f = probs * (d_probs - delta)
    d_q_scaled = nn(d_scores_f.astype(BF16), keys)
    query_unit = qu_v[...]
    grad = d_q_scaled * q_gain[...] * scale
    d_queries = qi_v[...] * (grad - query_unit * jnp.mean(grad * query_unit, axis=1, keepdims=True))
    dqa[z] = d_queries.astype(BF16)

    def pass_on(from_z, hops):
        remote(dqa.at[from_z], dqa.at[from_z], send.at[S_DQ], dq_recv.at[from_z],
               (dp, z_at(hops))).start()

    def arrived(from_z):
        remote(dqa.at[from_z], dqa.at[from_z], send.at[S_DQ], dq_recv.at[from_z],
               (dp, z_at(1))).wait_recv()

    for hops in (4, -4, 2, -2, 1, -1):
        pass_on(z, hops)

    d_scores = d_scores_f.astype(BF16).astype(F32).T.astype(BF16)
    probs_t = probs_low.astype(F32).T.astype(BF16)
    d_keys = nn(d_scores, q_scaled)
    d_values = nn(probs_t, d_attn)
    kgs[...] = jnp.concatenate(
        [d_keys.reshape(N, 8, W), d_values.reshape(N, 8, W)], axis=1
    ).astype(BF16)
    to_z(S_KVG, lambda to: kgs.at[to], kgr.at[z])
    kgr[z] = kgs[z]
    query_part = jnp.sum(d_q_scaled * query_unit, axis=0, keepdims=True) * scale

    wait_for(recv.at[S_QT2], qw_v.at[pl.ds(0, 7936)])

    def text_term(head):
        return nt(dqa[head], qt[lax.rem(head, 2), head // 2])

    acc[...] = text_term(z)

    def relay(k):
        for sign in (1, -1):
            near = z_at(-sign * (4 * k + 2))
            arrived(near)
            pass_on(near, sign)
        for sign in (1, -1):
            if k == 3 and sign == -1:
                continue
            far = z_at(-sign * (4 * k + 4))
            arrived(far)
            if k < 3:
                if not (k == 2 and sign == -1):
                    pass_on(far, 4 * sign)
                pass_on(far, 2 * sign)
                pass_on(far, sign)

    def use(k):
        total = acc[...]
        for j in (2, 4):
            for sign in (1, -1):
                if k == 3 and j == 4 and sign == -1:
                    continue
                total = total + text_term(z_at(-sign * (4 * k + j)))
        for j in (1, 3):
            for sign in (1, -1):
                from_z = z_at(-sign * (4 * k + j))
                arrived(from_z)
                total = total + text_term(from_z)
        acc[...] = total

    relay(0)
    relay(1)
    use(0)

    wait_for(recv.at[S_KVG], kgr.at[pl.ds(0, N - 1)])
    kv_sum = jnp.sum(kgr[...].astype(F32).reshape(4, 8, 16, W), axis=1)
    key_part = jnp.zeros((8, W), F32)
    for k in range(4):
        d_key = kv_sum[k, :8]
        key_unit = ku_v[k]
        key_part = key_part + d_key * key_unit
        key_grad = d_key * k_gain[...]
        dps[2 * k] = ki_v[k] * (
            key_grad - key_unit * jnp.mean(key_grad * key_unit, axis=1, keepdims=True)
        )
        dps[2 * k + 1] = kv_sum[k, 8:]
    to_plane(S_DPA, lambda to: dps.at[to // 4], dpr.at[dp])
    dpr[dp] = dps[dp // 4]
    key_part = jnp.sum(key_part, axis=0, keepdims=True)
    row8 = lax.broadcasted_iota(jnp.int32, (8, W), 0)
    gs[...] = jnp.where(
        row8 == 0, jnp.broadcast_to(query_part, (8, W)), jnp.broadcast_to(key_part, (8, W))
    )
    to_plane(S_G1, lambda to: gs, gr.at[dp])
    gr[dp] = gs[...]

    relay(2)
    use(1)

    wait_for(recv.at[S_DPA], dpr.at[pl.ds(0, N - 1)])
    d_plane = nn(dpr[...].reshape(256, W).astype(BF16), wf[:, :ENC])
    fs[...] = jnp.concatenate(
        [d_plane[:, :HALF].reshape(N, 8, HALF), d_plane[:, HALF:].reshape(N, 8, HALF)], axis=1
    ).astype(BF16)
    to_plane(S_FR, lambda to: fs.at[to], fr.at[dp])
    fr[dp] = fs[dp]

    wait_for(recv.at[S_G1], gr.at[pl.ds(0, N - 1)])
    gs2[...] = jnp.sum(gr[...], axis=0)
    to_z(S_G2, lambda to: gs2, gr2.at[z])
    gr2[z] = gs2[...]

    relay(3)
    use(2)

    wait_for(recv.at[S_FR], fr.at[pl.ds(0, N - 1)])
    back = jnp.sum(fr[...].astype(F32), axis=0)
    d_normed = jnp.concatenate([back[:8], back[8:]], axis=1)
    feat_grad = d_normed * enc_gain[...]
    unit = unit_v[...]
    feat_out[...] = (
        istd_v[:, :1]
        * (
            feat_grad
            - jnp.mean(feat_grad, axis=1, keepdims=True)
            - unit * jnp.mean(feat_grad * unit, axis=1, keepdims=True)
        )
    ).astype(BF16)

    use(3)
    text_out[...] = acc[...].astype(BF16)

    wait_for(recv.at[S_G2], gr2.at[pl.ds(0, N - 1)])
    gains = jnp.sum(gr2[...], axis=0)
    qg_out[...] = gains[0:1]
    kg_out[...] = gains[1:2]

    for s in range(16):
        copies = ring_copies(s)
        copies[0].wait_send()
        if s < 15:
            copies[1].wait_send()
    wait_for(send.at[S_NRM], nrm.at[pl.ds(0, N - 1)])
    wait_for(send.at[S_PLA], pp.at[pl.ds(0, N - 1)])
    wait_for(send.at[S_KV], kvr.at[pl.ds(0, N - 1)])
    wait_for(send.at[S_KVG], kgr.at[pl.ds(0, N - 1)])
    wait_for(send.at[S_DPA], dpr.at[pl.ds(0, N - 1)])
    wait_for(send.at[S_FR], fr.at[pl.ds(0, N - 1)])
    wait_for(send.at[S_G1], gr.at[pl.ds(0, N - 1)])
    wait_for(send.at[S_G2], gr2.at[pl.ds(0, N - 1)])
    wait_for(send.at[S_QT2], qw_v.at[pl.ds(0, 7936)])
    wait_for(send.at[S_DQ], dqa.at[pl.ds(0, N - 1)])

    @pl.when(owning)
    def _():
        wait_for(send.at[S_WRS], wr.at[pl.ds(0, TILES - 1)])
        wait_for(send.at[S_WAG], wr.at[pl.ds(0, N - 1)])

    @pl.when(jnp.logical_not(owning))
    def _():
        wait_for(send.at[S_WRS], wr.at[pl.ds(0, TILES)])

    @pl.when(even)
    def _():
        wait_for(send.at[S_QT1], kvr.at[pl.ds(0, N - 1)])


def on_device(
    text, q_weight, q_gain, enc_hidden, enc_branch, enc_gate, enc_gain, enc_bias,
    proj_weight, proj_bias, kv_weight, k_gain, attn_gate, o_weight, d_update,
    tile_counts, image_sample, text_lengths,
):
    vmem = pl.BlockSpec(memory_space=pltpu.VMEM)
    smem = pl.BlockSpec(memory_space=pltpu.SMEM)
    anywhere = pl.BlockSpec(memory_space=pl.ANY)
    scratch = [
        pltpu.VMEM((128, 8192), BF16), pltpu.VMEM((8192, W), BF16),
        pltpu.VMEM((ENC, 256), BF16), pltpu.VMEM((256, 1024), BF16),
        pltpu.VMEM((4096, 256), BF16),
        pltpu.VMEM((N, 16, HALF), BF16),
        pltpu.VMEM((W, AUG), BF16),
        pltpu.VMEM((N, 16, W), BF16),
        pltpu.VMEM((16, W), BF16),
        pltpu.VMEM((W, AUG), BF16),
        pltpu.VMEM((N, 8, W), F32), pltpu.VMEM((N, 8, W), F32),
        pltpu.VMEM((4, 16, W), BF16), pltpu.VMEM((N, 16, W), BF16),
        pltpu.VMEM((N, 16, W), BF16), pltpu.VMEM((N, 16, W), BF16),
        pltpu.VMEM((8, 8, W), F32), pltpu.VMEM((N, 8, W), F32),
        pltpu.VMEM((N, 16, HALF), BF16), pltpu.VMEM((N, 16, HALF), BF16),
        pltpu.VMEM((8, W), F32), pltpu.VMEM((N, 8, W), F32),
        pltpu.VMEM((8, W), F32), pltpu.VMEM((N, 8, W), F32),
        pltpu.VMEM((17, W, W), BF16), pltpu.VMEM((17, W, W), BF16),
        pltpu.VMEM((N, W, W), BF16),
        pltpu.VMEM((2, 16, 256, W), BF16),
        pltpu.VMEM((W, W), F32), pltpu.VMEM((W, W), BF16), pltpu.VMEM((W, W), F32),
        pltpu.VMEM((4, 8, W), F32), pltpu.VMEM((4, 8, W), F32),
        pltpu.VMEM((8, ENC), F32), pltpu.VMEM((8, W), F32),
        pltpu.VMEM((W, 256), F32),
        pltpu.SemaphoreType.DMA((5,)),
        pltpu.SemaphoreType.DMA((13,)), pltpu.SemaphoreType.DMA((13,)),
        pltpu.SemaphoreType.DMA((2, 16)), pltpu.SemaphoreType.DMA((2, 16)),
        pltpu.SemaphoreType.DMA((N,)),
    ]
    attn, d_text, d_features, d_q_gain, d_k_gain = pl.pallas_call(
        kernel,
        out_shape=(
            jax.ShapeDtypeStruct((128, W), BF16),
            jax.ShapeDtypeStruct((128, 256), BF16),
            jax.ShapeDtypeStruct((8, ENC), BF16),
            jax.ShapeDtypeStruct((1, W), F32),
            jax.ShapeDtypeStruct((1, W), F32),
        ),
        in_specs=[smem] * 5 + [vmem] * 8 + [anywhere] * 5,
        out_specs=(vmem,) * 5,
        scratch_shapes=scratch,
        compiler_params=pltpu.CompilerParams(
            collective_id=0, has_side_effects=True, vmem_limit_bytes=40 << 20
        ),
        name="layer",
    )(
        tile_counts, image_sample, text_lengths, enc_gate.reshape(1, 1), attn_gate.reshape(1, 1),
        q_gain.reshape(1, W), k_gain.reshape(1, W), enc_hidden, enc_branch,
        enc_gain.reshape(1, ENC), enc_bias.reshape(1, ENC), proj_bias.reshape(1, 256), d_update,
        text, q_weight, proj_weight, kv_weight, o_weight,
    )
    return attn, d_text, d_features, d_q_gain.reshape(W), d_k_gain.reshape(W)


def solution(mesh):
    in_specs = (
        P("dp", None),
        P(None, "head"),
        P(),
        P(("dp", "head"), None),
        P(("dp", "head"), None),
        P(),
        P(),
        P(),
        P(None, "head"),
        P("head"),
        P("head", None),
        P(),
        P(),
        P(None, "head"),
        P("dp", "head"),
        P("dp", None),
        P("dp", None),
        P("dp", None),
    )
    out_specs = (P("dp", "head"), P("dp", "head"), P(("dp", "head"), None), P(), P())
    return jax.shard_map(
        on_device, mesh=mesh, in_specs=in_specs, out_specs=out_specs, check_vma=False
    )
```

time: 846 us -> 177 us (0.21)
  waiting for transfers between devices: 503 us -> 0 us
  blocking collectives: 278 us -> 0 us
  Pallas kernels: 0 us -> 154 us
  matrix products: 20.1 us -> 0 us
  starting transfers between devices: 17.2 us -> 0 us
  between operations: 15.6 us -> 1.95 us
  local copies, waits for them, and re-layouts: 4.45 us -> 17.4 us
    psum x1 -> x0, waiting for transfers between devices: 251 us -> none  [on_device(): lax.psum(jnp.dot(proj_feat, kv_weight, preferred_element_type=jnp.float32...]
    reduce_scatter x3 -> x0, waiting for transfers between devices: 226 us -> none  [the longest x1 129 us: on_device(): lax.psum_scatter(partial_terms, 'head', scatter_dimension=1, tiled=True)]
    pallas_call x0 -> x1, Pallas kernels: none -> 154 us  [on_device(): pl.pallas_call(kernel, out_shape=(jax.ShapeDtypeStruct((128, W), BF16), j...]
    psum x1 -> x0, blocking collectives: 152 us -> none  [on_device(): d_q_gain, d_k_gain = lax.psum((query_part, key_part), ('dp', 'head'))]
    all_gather x2 -> x0, blocking collectives: 126 us -> none  [the longest x1 71.5 us: on_device(): lax.all_gather(normed, 'head', axis=0, tiled=True)]
    all_to_all x1 -> x0, waiting for transfers between devices: 26.6 us -> none  [on_device(): lax.all_to_all(kv_grads, 'head', split_axis=0, concat_axis=1, tiled=True)]
    dot_general x11 -> x0, matrix products: 20.1 us -> none  [the longest x1 3.75 us: on_device(): jnp.einsum('tf,cf->tc', d_update, o_weight, preferred_element_type=jnp.fl...]
    all_to_all x1 -> x0, starting transfers between devices: 17.1 us -> none  [on_device(): lax.all_to_all(kv_grads, 'head', split_axis=0, concat_axis=1, tiled=True)]
  transfers between devices with their start and end apart: 5 -> 0, of which waited for: 4 -> 0; matrix products, arithmetic and copies ran while one was open for 2% -> 0% of each run, Pallas kernels for 0% -> 0%
where the time goes in v1:
time: 177 us; the launch traced here: 174 us
  Pallas kernels  154 us (87%)
  local copies, waits for them, and re-layouts  17.4 us (10%)
  between operations  1.95 us (1%)
    pallas_call x1, Pallas kernels, on_device(): pl.pallas_call(kernel, out_shape=(jax.ShapeDtypeStruct((128, W), BF16), j...  154 us
    unnamed x33, local copies, waits for them, and re-layouts  16 us

profile of v1, /device:TPU:6, one launch (start us, length us, event | category | flops | bytes accessed | tf_op | source)
XLA Modules:
  0.0 173.5 jit_solution(7416699012004309816)
XLA Ops:
  1.9 0.7 reshape.41.enc_gain
  2.6 0.7 reshape.42.enc_bias
  3.3 0.0 copy-start
  3.3 1.6 copy-done
  4.9 0.0 copy-start.1
  4.9 1.6 copy-done.1
  6.5 0.0 copy-start.2
  6.5 1.6 copy-done.2
  8.1 0.0 copy-start.3
  8.1 1.1 copy-done.3
  9.2 0.0 copy-start.4
  9.2 1.0 copy-done.4
  10.2 0.0 copy-start.5
  10.2 0.8 copy-done.5
  11.1 0.0 copy-start.6
  11.1 0.7 copy-done.6
  11.8 0.0 copy-start.7
  11.8 0.7 copy-done.7
  12.5 0.0 copy-start.8
  12.5 0.7 copy-done.8
  13.2 0.0 copy-start.9
  13.2 0.7 copy-done.9
  13.9 0.0 copy-start.10
  13.9 0.7 copy-done.10
  14.5 0.0 copy-start.11
  14.5 0.7 copy-done.11
  15.2 0.0 copy-start.12
  15.2 0.7 copy-done.12
  15.8 0.0 copy-start.13
  15.8 0.7 copy-done.13
  16.5 154.2 %layer.1 = (bf16[128,128]{1,0:T(8,128)(2,1)S(1)}, bf16[128,256]{1,0:T(8,128)(2,1)S(1)}, bf16[8,1280]{1,0:T(8,128)(2,1)S(1)}, f32[1,128]{1,0:T(1,128)S(1)}, f32[1,128]{1,0:T(1,128)S(1)}) custom-call(s32[1,3]{1,0:T(1,128)S(1)} %copy-done.9, s32[1,3]{1,0:T(1,128)S(1)} %copy-done.10, s32[1,2]{1,0:T(1,128)S(1)} %copy-done.11, f32[1,1]{1,0:T(1,128)} %bitcast.7.enc_gate, ...), custom_call_target="tpu_custom_call" | custom-call | tf_op jit(solution)/shard_map/layer/pallas_call | solution.py:496
  170.7 0.6 copy.30
  171.3 0.6 copy.31
  171.9 0.6 copy.32
  172.5 0.5 copy.33
  173.0 0.5 copy.34
Async XLA Ops:
  3.3 1.6 copy-start
  4.9 1.6 copy-start.1
  6.5 1.6 copy-start.2
  8.1 1.1 copy-start.3
  9.2 1.0 copy-start.4
  10.2 0.8 copy-start.5
  11.1 0.7 copy-start.6
  11.8 0.7 copy-start.7
  12.5 0.7 copy-start.8
  13.2 0.7 copy-start.9
  13.9 0.7 copy-start.10
  14.5 0.7 copy-start.11
  15.2 0.7 copy-start.12
  15.8 0.7 copy-start.13

commit v2 on v1

v2 whole, which is shorter than its diff:
```python
import jax
import jax.numpy as jnp
from jax import lax
from jax.experimental import pallas as pl
from jax.experimental.pallas import tpu as pltpu
from jax.sharding import PartitionSpec as P

N = 32
TXT = 64
TILE = 32
W = 128
ENC = 1280
HALF = 640
AUG = 1408
TILES = 22
EPSILON = 1e-05
MESH = pl.DeviceIdType.MESH
F32 = jnp.float32
BF16 = jnp.bfloat16

(
    S_NRM, S_WRS, S_WAG, S_PLA, S_KV, S_KG1, S_KG2, S_G1, S_G2, S_QT1, S_QT2, S_QT3, S_WG1, S_WG2, S_DQ, S_C,
) = range(16)


def nn(a, b):
    return lax.dot_general(a, b, (((1,), (0,)), ((), ())), preferred_element_type=F32)


def nt(a, b):
    return lax.dot_general(a, b, (((1,), (1,)), ((), ())), preferred_element_type=F32)


def tn(a, b):
    return lax.dot_general(a, b, (((0,), (0,)), ((), ())), preferred_element_type=F32)


def kernel(
    enc_hidden_h, enc_branch_h, enc_gate_h, enc_gain_h, enc_bias_h, proj_weight, kv_weight, proj_bias_h,
    d_update_h, o_weight, tiles_h, owners_h, lengths_h, attn_gate_h, q_gain_h, k_gain_h,
    q_weight, text,
    attn_out, text_out, feat_out, qg_out, kg_out,
    enc_hidden, enc_branch, enc_gate, enc_gain, enc_bias, pw_v, kvw_v, proj_bias,
    d_update, ow_v, tiles, owners, lengths, attn_gate, q_gain, k_gain, qw_v, text_v,
    nrm, wt, wr, ws, wf, wg, pp, pr, kvs, kvr, kgs, kg1, kg2, kgr,
    gs, gr, gs2, gr2, terms, rx1, rx2, dqa, qt,
    qu_v, qs_v, qi_v, ku_v, ki_v, unit_v, istd_v, acc,
    load_sem, send, recv, c1_recv, c2_recv, dq_recv,
):
    dp = lax.axis_index("dp")
    z = lax.axis_index("head")

    def z_at(k):
        return lax.rem(z + k + 2 * N, N)

    def remote(src, dst, s_sem, r_sem, dev):
        return pltpu.make_async_remote_copy(
            src_ref=src, dst_ref=dst, send_sem=s_sem, recv_sem=r_sem,
            device_id=dev, device_id_type=MESH,
        )

    def wait_for(sem, ref):
        pltpu.make_async_copy(ref, ref, sem).wait()

    def far_first(n):
        step = (n + 1) // 2
        return jnp.where(lax.rem(n, 2) == 1, 16 + step, 16 - step)

    def to_z(stage, src_of, dst):
        def one(n, _):
            to = z_at(far_first(n))
            remote(src_of(to), dst, send.at[stage], recv.at[stage], (dp, to)).start()
            return 0
        lax.fori_loop(0, N - 1, one, 0)

    def to_plane(stage, src_of, dst):
        def one(n, _):
            to = lax.rem(dp + far_first(n), N)
            remote(src_of(to), dst, send.at[stage], recv.at[stage], (to, z)).start()
            return 0
        lax.fori_loop(0, N - 1, one, 0)

    loads = [
        pltpu.make_async_copy(src, dst, load_sem.at[n])
        for n, (src, dst) in enumerate((
            (kv_weight, kvw_v), (proj_weight, pw_v), (proj_bias_h, proj_bias),
            (enc_hidden_h, enc_hidden), (enc_branch_h, enc_branch), (enc_gate_h, enc_gate),
            (enc_gain_h, enc_gain), (enc_bias_h, enc_bias), (d_update_h, d_update),
            (o_weight, ow_v), (tiles_h, tiles), (owners_h, owners), (lengths_h, lengths),
            (attn_gate_h, attn_gate), (q_gain_h, q_gain), (k_gain_h, k_gain),
            (q_weight, qw_v), (text, text_v),
        ))
    ]
    for load in loads:
        load.start()
    wf[...] = jnp.zeros_like(wf)

    barrier = pltpu.get_barrier_semaphore()

    def greet(k, _):
        pl.semaphore_signal(barrier, inc=1, device_id=(dp, z_at(k)), device_id_type=MESH)
        pl.semaphore_signal(
            barrier, inc=1, device_id=(lax.rem(dp + k, N), z), device_id_type=MESH
        )
        return 0

    lax.fori_loop(1, N, greet, 0)

    block = dp // 4
    quarter = lax.rem(dp, 4)
    rows0 = 32 * quarter
    for load in loads[:3]:
        load.wait()
    kv_t = kvw_v[:, pl.ds(pl.multiple_of(W * block, W), W)].astype(F32).T.astype(BF16)
    wt[:, :ENC] = nt(kv_t, pw_v[...]).astype(BF16)
    first_row = lax.broadcasted_iota(jnp.int32, (W, 256), 0) == 0
    bias_rows = jnp.where(first_row, jnp.broadcast_to(proj_bias[...], (W, 256)), 0.0).astype(BF16)
    wt[:, ENC:] = nt(kv_t, bias_rows).astype(BF16)

    def tile_of(ref, t):
        row = pl.multiple_of(rows0 + 16 * (t // 11), 16)
        col = pl.multiple_of(W * lax.rem(t, 11), W)
        return ref.at[pl.ds(row, 16), pl.ds(col, W)]

    own_tile = (11 * z + 15) // 16
    owning = jnp.logical_and(own_tile < TILES, (16 * own_tile) // 11 == z)

    pl.semaphore_wait(barrier, 2 * (N - 1))

    def send_tile(n, _):
        t = lax.rem((11 * z_at(16) + 15) // 16 + n, TILES)
        to = (16 * t) // 11

        @pl.when(to != z)
        def _():
            remote(tile_of(wt, t), wr.at[z], send.at[S_WRS], recv.at[S_WRS], (dp, to)).start()
        return 0

    lax.fori_loop(0, TILES, send_tile, 0)

    for load in loads[3:8]:
        load.wait()
    gate = jnp.tanh(enc_gate[...])
    gain_row = jnp.concatenate([enc_gain[n : n + 1] for n in range(10)], axis=1)
    bias_row = jnp.concatenate([enc_bias[n : n + 1] for n in range(10)], axis=1)
    features = enc_hidden[...].astype(F32) + gate * enc_branch[...].astype(F32)
    centered = features - jnp.mean(features, axis=1, keepdims=True)
    inv_std = lax.rsqrt(jnp.mean(centered * centered, axis=1, keepdims=True) + EPSILON)
    unit = centered * inv_std
    unit_v[...] = unit
    istd_v[...] = jnp.broadcast_to(inv_std, (8, W))
    normed = unit * gain_row + bias_row
    nrm[dp] = jnp.concatenate([normed[:, :HALF], normed[:, HALF:]], axis=0).astype(BF16)

    to_plane(S_NRM, lambda to: nrm.at[dp], nrm.at[dp])

    for load in loads[8:10]:
        load.wait()
    for n in range(4):
        heads = nt(d_update[...], ow_v[1024 * n : 1024 * (n + 1)]).astype(BF16)
        for j in range(8):
            terms[8 * n + j] = heads[:, W * j : W * (j + 1)]

    sides = ((0, 1), (1, -1))

    def first_terms():
        remote(terms.at[z_at(16)], rx2.at[0, 7], send.at[S_C], c2_recv.at[0, 7],
               (dp, z_at(2))).start()

        def one(n, _):
            j = 7 - n
            for side, sign in sides:
                remote(terms.at[z_at(sign * (2 * j + 1))], rx1.at[side, j], send.at[S_C],
                       c1_recv.at[side, j], (dp, z_at(sign))).start()
            return 0
        lax.fori_loop(0, 8, one, 0)

    def reached(side, j, long):
        remote(terms.at[z], rx1.at[side, j], send.at[S_C], c1_recv.at[side, j],
               (dp, z_at(1))).wait_recv()
        total = rx1[side, j].astype(F32)
        if long:
            remote(terms.at[z], rx2.at[side, j], send.at[S_C], c2_recv.at[side, j],
                   (dp, z_at(1))).wait_recv()
            total = total + rx2[side, j].astype(F32)
        return total

    def send_on(side, sign, j, long):
        at = z_at(sign * 2 * j)
        terms[at] = (terms[at].astype(F32) + reached(side, j, long)).astype(BF16)
        remote(terms.at[at], rx2.at[side, j - 1], send.at[S_C], c2_recv.at[side, j - 1],
               (dp, z_at(2 * sign))).start()

    def next_terms(high, low):
        def one(n, _):
            for side, sign in sides:
                send_on(side, sign, high - n, True)
            return 0
        lax.fori_loop(0, high - low + 1, one, 0)

    chip = dp // 2
    core = lax.rem(dp, 2)

    def to_chips(stage, src, dst):
        def one(n, _):
            to = lax.rem(dp + 2 * n, N)
            remote(src, dst, send.at[stage], recv.at[stage], (to, z)).start()
            return 0
        lax.fori_loop(1, 16, one, 0)

    def to_sibling(stage, ref):
        remote(ref, ref, send.at[stage], recv.at[stage], (dp + 1 - 2 * core, z)).start()

    first_terms()

    for load in loads[10:]:
        load.wait()
    query_pre = nn(text_v[...], qw_v[...])
    inv_query = lax.rsqrt(jnp.mean(query_pre * query_pre, axis=1, keepdims=True) + EPSILON)
    scale = W ** (-0.5)
    query_unit = query_pre * inv_query
    qu_v[...] = query_unit
    qi_v[...] = jnp.broadcast_to(inv_query, (W, W))
    qs_v[...] = (query_unit * q_gain[...] * scale).astype(BF16)

    send_on(1, -1, 7, False)
    send_on(0, 1, 7, True)
    next_terms(6, 6)

    @pl.when(owning)
    def _():
        wait_for(recv.at[S_WRS], wr.at[pl.ds(0, N - 1)])
        wr[z] = tile_of(wt, own_tile)[...]
        tile = jnp.sum(wr[...].astype(F32), axis=0).astype(BF16)
        ws[...] = tile
        tile_of(wf, own_tile)[...] = tile
        to_z(S_WAG, lambda to: ws, tile_of(wf, own_tile))

    part = pl.ds(pl.multiple_of(16 * chip, 16), 16)
    even = lax.rem(z, 2) == core

    @pl.when(even)
    def _():
        to_z(
            S_QT1,
            lambda to: qw_v.at[pl.ds(pl.multiple_of(256 * to + 16 * chip, 16), 16)],
            qt.at[core, z // 2, part],
        )
        qt[core, z // 2, part] = qw_v[pl.ds(pl.multiple_of(256 * z + 16 * chip, 16), 16)]

    next_terms(5, 3)

    @pl.when(owning)
    def _():
        wait_for(recv.at[S_WAG], wr.at[pl.ds(0, TILES - 1)])

    @pl.when(jnp.logical_not(owning))
    def _():
        wait_for(recv.at[S_WAG], wr.at[pl.ds(0, TILES)])

    wait_for(recv.at[S_NRM], nrm.at[pl.ds(0, N - 1)])

    plane = nrm[...].reshape(2 * 256, HALF)
    half_a = nt(plane, wf[:, :HALF]).reshape(N, 16, W)
    half_b = nt(plane, wf[:, HALF:ENC]).reshape(N, 16, W)
    ones = jnp.where(lax.broadcasted_iota(jnp.int32, (8, W), 1) == 0, 1.0, 0.0).astype(BF16)
    bias = nt(ones, wf[:, ENC:])
    pp[...] = half_a[:, :8] + half_b[:, 8:] + bias[None]
    to_plane(S_PLA, lambda to: pp.at[to], pr.at[dp])
    pr[dp] = pp[dp]

    own_rows = wf.at[pl.ds(pl.multiple_of(rows0, 32), 32), pl.ds(0, ENC)]
    wg[chip, core] = own_rows[...]

    @pl.when(even)
    def _():
        wait_for(recv.at[S_QT1], kvr.at[pl.ds(0, 15)])

    @pl.when(jnp.logical_not(even))
    def _():
        wait_for(recv.at[S_QT1], kvr.at[pl.ds(0, 16)])

    to_chips(S_QT2, qt.at[core, :, part], qt.at[core, :, part])


    next_terms(2, 2)

    wait_for(recv.at[S_PLA], pr.at[pl.ds(0, N - 1)])
    blocks = jnp.sum(pr[...].reshape(8, 4, 8, W), axis=1)
    for k in range(4):
        key_pre = blocks[2 * k]
        inv_key = lax.rsqrt(jnp.mean(key_pre * key_pre, axis=1, keepdims=True) + EPSILON)
        key_unit = key_pre * inv_key
        ku_v[k] = key_unit
        ki_v[k] = jnp.broadcast_to(inv_key, (8, W))
        kvs[k] = jnp.concatenate([key_unit * k_gain[...], blocks[2 * k + 1]], axis=0).astype(BF16)
    to_z(S_KV, lambda to: kvs.at[to // 8], kvr.at[z])
    kvr[z] = kvs[z // 8]
    to_chips(S_WG1, wg.at[chip, core], wg.at[chip, core])

    next_terms(1, 1)

    row = lax.broadcasted_iota(jnp.int32, (W, 256), 1)
    slot = lax.broadcasted_iota(jnp.int32, (W, 256), 0)
    end0 = tiles[:, 0:1] * TILE
    end1 = end0 + tiles[:, 1:2] * TILE
    key_sample = jnp.where(
        row < end0, owners[:, 0:1], jnp.where(row < end1, owners[:, 1:2], owners[:, 2:3])
    )
    allowed = jnp.where((slot >= TXT).astype(jnp.int32) == key_sample, 1.0, 0.0)
    slot_w = lax.broadcasted_iota(jnp.int32, (W, W), 0)
    limit = jnp.where(slot_w >= TXT, lengths[:, 1:2] + TXT, lengths[:, 0:1])
    valid = jnp.where(slot_w < limit, 1.0, 0.0)
    attn_total = terms[z].astype(F32) + reached(0, 0, True) + reached(1, 0, True)
    d_gate = jnp.tanh(attn_gate[...])
    d_attn = (d_gate * attn_total * valid).astype(BF16)

    wait_for(recv.at[S_QT2], qt.at[0, pl.ds(0, 15)])
    to_sibling(S_QT3, qt.at[core])

    wait_for(recv.at[S_KV], kvr.at[pl.ds(0, N - 1)])
    kv_f = kvr[...].astype(F32)
    keys = kv_f[:, :8].reshape(256, W).astype(BF16)
    values = kv_f[:, 8:].reshape(256, W).astype(BF16)
    q_scaled = qs_v[...]
    weighted = jnp.exp(nt(q_scaled, keys)) * allowed
    probs = weighted / jnp.sum(weighted, axis=1, keepdims=True)
    probs_low = probs.astype(BF16)

    d_probs = nt(d_attn, values)
    delta = jnp.sum(d_probs * probs, axis=1, keepdims=True)
    d_scores_f = probs * (d_probs - delta)
    d_q_scaled = nn(d_scores_f.astype(BF16), keys)
    query_unit = qu_v[...]
    grad = d_q_scaled * q_gain[...] * scale
    d_queries = qi_v[...] * (grad - query_unit * jnp.mean(grad * query_unit, axis=1, keepdims=True))
    dqa[z] = d_queries.astype(BF16)

    def pass_on(from_z, hops):
        remote(dqa.at[from_z], dqa.at[from_z], send.at[S_DQ], dq_recv.at[from_z],
               (dp, z_at(hops))).start()

    def arrived(from_z):
        remote(dqa.at[from_z], dqa.at[from_z], send.at[S_DQ], dq_recv.at[from_z],
               (dp, z_at(1))).wait_recv()

    for hops in (3, -3, 1, -1):
        pass_on(z, hops)

    attn_out[...] = (nn(probs_low, values) * valid).astype(BF16)
    d_scores = d_scores_f.astype(BF16).astype(F32).T.astype(BF16)
    probs_t = probs_low.astype(F32).T.astype(BF16)
    d_keys = nn(d_scores, q_scaled)
    query_part = jnp.sum(d_q_scaled * query_unit, axis=0, keepdims=True) * scale
    key_part = jnp.sum(
        d_keys.astype(BF16).astype(F32) * keys.astype(F32), axis=0, keepdims=True
    ) / k_gain[...]
    gs[...] = jnp.concatenate([query_part, key_part], axis=0)
    to_plane(S_G1, lambda to: gs, gr.at[dp])
    gr[dp] = gs[...]

    d_values = nn(probs_t, d_attn)
    kgs[...] = jnp.concatenate(
        [d_keys.reshape(N, 8, W), d_values.reshape(N, 8, W)], axis=1
    ).astype(BF16)
    seg = z // 8
    place = lax.rem(z, 8)

    def to_segment(n, _):
        to = lax.rem(place + n, 8)
        remote(kgs.at[pl.ds(4 * to, 4)], kg1.at[place], send.at[S_KG1], recv.at[S_KG1],
               (dp, 8 * seg + to)).start()
        return 0

    lax.fori_loop(1, 8, to_segment, 0)
    kg1[place] = kgs[pl.ds(4 * place, 4)]
    wait_for(recv.at[S_WG1], wg.at[pl.ds(0, 15), 0])
    to_sibling(S_WG2, wg.at[:, core])

    def text_term(head):
        return nt(dqa[head], qt[lax.rem(head, 2), head // 2])

    ways = ((1, 16), (-1, 15))

    def relay(m):
        for sign, most in ways:
            if 3 * m + 1 > most:
                continue
            near = z_at(-sign * (3 * m + 1))
            arrived(near)
            if 3 * m + 2 <= most:
                pass_on(near, sign)
        if m == 5:
            return
        for sign, most in ways:
            far = z_at(-sign * (3 * m + 3))
            arrived(far)
            if 3 * m + 6 <= most:
                pass_on(far, 3 * sign)
            if 3 * m + 4 <= most:
                pass_on(far, sign)

    def use(m):
        heads = []
        for j in (1, 3, 2):
            for sign, most in ways:
                if 3 * m + j <= most:
                    heads.append(z_at(-sign * (3 * m + j)))
                    if j == 2:
                        arrived(heads[-1])
        acc[...] = acc[...] + nt(
            jnp.concatenate([dqa[h] for h in heads], axis=1),
            jnp.concatenate([qt[lax.rem(h, 2), h // 2] for h in heads], axis=1),
        )

    relay(0)

    wait_for(recv.at[S_KG1], kg1.at[pl.ds(0, 7)])
    kg2[...] = jnp.sum(kg1[...].astype(F32), axis=0).astype(BF16)
    for j in range(4):
        to_owner = 4 * place + j

        @pl.when(to_owner != z)
        def _():
            remote(kg2.at[j], kgr.at[seg], send.at[S_KG2], recv.at[S_KG2], (dp, to_owner)).start()

        @pl.when(to_owner == z)
        def _():
            kgr[seg] = kg2[j]

    wait_for(recv.at[S_G1], gr.at[pl.ds(0, N - 1)])
    gs2[...] = jnp.sum(gr[...], axis=0)
    to_z(S_G2, lambda to: gs2, gr2.at[z])
    gr2[z] = gs2[...]

    wait_for(recv.at[S_QT3], qt.at[0])
    acc[...] = text_term(z)

    relay(1)
    use(0)
    relay(2)
    use(1)
    relay(3)
    use(2)
    relay(4)
    use(3)

    summing = 4 * place <= z
    summing = jnp.logical_and(summing, z < 4 * place + 4)

    @pl.when(summing)
    def _():
        wait_for(recv.at[S_KG2], kgr.at[pl.ds(0, 3)])

    @pl.when(jnp.logical_not(summing))
    def _():
        wait_for(recv.at[S_KG2], kgr)

    kv_sum = kgr[...].astype(F32)
    d_projected = []
    for k in range(4):
        key_unit = ku_v[k]
        key_grad = kv_sum[k, :8] * k_gain[...]
        d_projected.append(ki_v[k] * (
            key_grad - key_unit * jnp.mean(key_grad * key_unit, axis=1, keepdims=True)
        ))
        d_projected.append(kv_sum[k, 8:])
    wait_for(recv.at[S_WG2], wg.at[:, 0])
    d_normed = nn(
        jnp.concatenate(d_projected, axis=1).astype(BF16), wg[...].reshape(1024, ENC)
    )
    feat_grad = d_normed * jnp.concatenate([enc_gain[n : n + 1] for n in range(10)], axis=1)
    unit = unit_v[...]
    feat_out[...] = (
        istd_v[:, :1]
        * (
            feat_grad
            - jnp.mean(feat_grad, axis=1, keepdims=True)
            - unit * jnp.mean(feat_grad * unit, axis=1, keepdims=True)
        )
    ).astype(BF16)

    use(4)
    relay(5)
    use(5)
    text_out[...] = acc[...].astype(BF16)

    wait_for(recv.at[S_G2], gr2.at[pl.ds(0, N - 1)])
    gains = jnp.sum(gr2[...], axis=0)
    qg_out[...] = gains[0:1]
    kg_out[...] = gains[1:2]

    wait_for(send.at[S_C], terms.at[pl.ds(0, N - 1)])
    wait_for(send.at[S_NRM], nrm.at[pl.ds(0, N - 1)])
    wait_for(send.at[S_PLA], pp.at[pl.ds(0, N - 1)])
    wait_for(send.at[S_KV], kvr.at[pl.ds(0, N - 1)])
    wait_for(send.at[S_KG1], kg1.at[pl.ds(0, 7)])
    wait_for(send.at[S_G1], gr.at[pl.ds(0, N - 1)])
    wait_for(send.at[S_G2], gr2.at[pl.ds(0, N - 1)])
    wait_for(send.at[S_QT2], qt.at[0, pl.ds(0, 15)])
    wait_for(send.at[S_QT3], qt.at[0])
    wait_for(send.at[S_WG1], wg.at[pl.ds(0, 15), 0])
    wait_for(send.at[S_WG2], wg.at[:, 0])
    wait_for(send.at[S_DQ], dqa.at[pl.ds(0, N - 1)])

    @pl.when(summing)
    def _():
        wait_for(send.at[S_KG2], kgr.at[pl.ds(0, 3)])

    @pl.when(jnp.logical_not(summing))
    def _():
        wait_for(send.at[S_KG2], kgr)

    @pl.when(owning)
    def _():
        wait_for(send.at[S_WRS], wr.at[pl.ds(0, TILES - 1)])
        wait_for(send.at[S_WAG], wr.at[pl.ds(0, N - 1)])

    @pl.when(jnp.logical_not(owning))
    def _():
        wait_for(send.at[S_WRS], wr.at[pl.ds(0, TILES)])

    @pl.when(even)
    def _():
        wait_for(send.at[S_QT1], kvr.at[pl.ds(0, N - 1)])


def on_device(
    text, q_weight, q_gain, enc_hidden, enc_branch, enc_gate, enc_gain, enc_bias,
    proj_weight, proj_bias, kv_weight, k_gain, attn_gate, o_weight, d_update,
    tile_counts, image_sample, text_lengths,
):
    vmem = pl.BlockSpec(memory_space=pltpu.VMEM)
    anywhere = pl.BlockSpec(memory_space=pl.ANY)
    arguments = (
        enc_hidden, enc_branch, enc_gate.reshape(1, 1), enc_gain.reshape(10, W),
        enc_bias.reshape(10, W), proj_weight, kv_weight, proj_bias.reshape(1, 256),
        d_update, o_weight, tile_counts, image_sample, text_lengths, attn_gate.reshape(1, 1),
        q_gain.reshape(1, W), k_gain.reshape(1, W), q_weight, text,
    )
    scratch = [pltpu.VMEM(a.shape, a.dtype) for a in arguments] + [
        pltpu.VMEM((N, 16, HALF), BF16),
        pltpu.VMEM((W, AUG), BF16),
        pltpu.VMEM((N, 16, W), BF16),
        pltpu.VMEM((16, W), BF16),
        pltpu.VMEM((W, AUG), BF16),
        pltpu.VMEM((16, 2, 32, ENC), BF16),
        pltpu.VMEM((N, 8, W), F32), pltpu.VMEM((N, 8, W), F32),
        pltpu.VMEM((4, 16, W), BF16), pltpu.VMEM((N, 16, W), BF16),
        pltpu.VMEM((N, 16, W), BF16), pltpu.VMEM((8, 4, 16, W), BF16),
        pltpu.VMEM((4, 16, W), BF16), pltpu.VMEM((4, 16, W), BF16),
        pltpu.VMEM((2, W), F32), pltpu.VMEM((N, 2, W), F32),
        pltpu.VMEM((2, W), F32), pltpu.VMEM((N, 2, W), F32),
        pltpu.VMEM((N, W, W), BF16),
        pltpu.VMEM((2, 8, W, W), BF16), pltpu.VMEM((2, 8, W, W), BF16),
        pltpu.VMEM((N, W, W), BF16),
        pltpu.VMEM((2, 16, 256, W), BF16),
        pltpu.VMEM((W, W), F32), pltpu.VMEM((W, W), BF16), pltpu.VMEM((W, W), F32),
        pltpu.VMEM((4, 8, W), F32), pltpu.VMEM((4, 8, W), F32),
        pltpu.VMEM((8, ENC), F32), pltpu.VMEM((8, W), F32),
        pltpu.VMEM((W, 256), F32),
        pltpu.SemaphoreType.DMA((len(arguments),)),
        pltpu.SemaphoreType.DMA((16,)), pltpu.SemaphoreType.DMA((16,)),
        pltpu.SemaphoreType.DMA((2, 8)), pltpu.SemaphoreType.DMA((2, 8)),
        pltpu.SemaphoreType.DMA((N,)),
    ]
    attn, d_text, d_features, d_q_gain, d_k_gain = pl.pallas_call(
        kernel,
        out_shape=(
            jax.ShapeDtypeStruct((128, W), BF16),
            jax.ShapeDtypeStruct((128, 256), BF16),
            jax.ShapeDtypeStruct((8, ENC), BF16),
            jax.ShapeDtypeStruct((1, W), F32),
            jax.ShapeDtypeStruct((1, W), F32),
        ),
        in_specs=[anywhere] * len(arguments),
        out_specs=(vmem,) * 5,
        scratch_shapes=scratch,
        compiler_params=pltpu.CompilerParams(
            collective_id=0, has_side_effects=True, vmem_limit_bytes=60 << 20
        ),
        name="layer",
    )(*arguments)
    return attn, d_text, d_features, d_q_gain.reshape(W), d_k_gain.reshape(W)


def solution(mesh):
    in_specs = (
        P("dp", None),
        P(None, "head"),
        P(),
        P(("dp", "head"), None),
        P(("dp", "head"), None),
        P(),
        P(),
        P(),
        P(None, "head"),
        P("head"),
        P("head", None),
        P(),
        P(),
        P(None, "head"),
        P("dp", "head"),
        P("dp", None),
        P("dp", None),
        P("dp", None),
    )
    out_specs = (P("dp", "head"), P("dp", "head"), P(("dp", "head"), None), P(), P())
    return jax.shard_map(
        on_device, mesh=mesh, in_specs=in_specs, out_specs=out_specs, check_vma=False
    )
```

time: 177 us -> 148 us (0.84); the launches traced: 174 us -> 148 us
  Pallas kernels: 154 us -> 139 us
  local copies, waits for them, and re-layouts: 17.4 us -> 6.52 us
    pallas_call x1, Pallas kernels: 154 us -> 139 us  [on_device(): pl.pallas_call(kernel, out_shape=(jax.ShapeDtypeStruct((128, W), BF16), j...]
    unnamed x33 -> x5, local copies, waits for them, and re-layouts: 16 us -> 6.52 us
where the time goes in v2:
time: 148 us
  Pallas kernels  139 us (94%)
  local copies, waits for them, and re-layouts  6.52 us (4%)
  between operations  1.94 us (1%)
    pallas_call x1, Pallas kernels, on_device(): pl.pallas_call(kernel, out_shape=(jax.ShapeDtypeStruct((128, W), BF16), j...  139 us
    unnamed x5, local copies, waits for them, and re-layouts  6.52 us

profile of v2, /device:TPU:6, one launch (start us, length us, event | category | flops | bytes accessed | tf_op | source)
XLA Modules:
  0.0 147.8 jit_solution(6795944253848569950)
XLA Ops:
  1.9 139.3 %layer.1 = (bf16[128,128]{1,0:T(8,128)(2,1)}, bf16[128,256]{1,0:T(8,128)(2,1)}, bf16[8,1280]{1,0:T(8,128)(2,1)}, f32[1,128]{1,0:T(1,128)}, f32[1,128]{1,0:T(1,128)}) custom-call(bf16[8,1280]{1,0:T(8,128)(2,1)} %enc_hidden_h.1, bf16[8,1280]{1,0:T(8,128)(2,1)} %enc_branch_h.1, f32[1,1]{1,0:T(1,128)} %bitcast.9.enc_gate_h, f32[10,128]{1,0:T(8,128)} %bitcast.11, ...), custom_call_target="tpu_custom_call" | custom-call | tf_op jit(solution)/shard_map/layer/pallas_call | solution.py:567
  141.2 1.4 copy.30
  142.6 1.5 copy.31
  144.1 1.3 copy.32
  145.4 1.2 copy.33
  146.6 1.2 copy.34

commit v3 on v2

--- a/solution.py
+++ b/solution.py
@@ -138,6 +138,63 @@
 
     lax.fori_loop(0, TILES, send_tile, 0)
 
+    for load in loads[8:10]:
+        load.wait()
+    for n in range(4):
+        heads = nt(d_update[...], ow_v[1024 * n : 1024 * (n + 1)]).astype(BF16)
+        for j in range(8):
+            terms[8 * n + j] = heads[:, W * j : W * (j + 1)]
+
+    sides = ((0, 1), (1, -1))
+
+    def odd_terms(high, low):
+        def one(n, _):
+            j = high - n
+            for side, sign in sides:
+                remote(terms.at[z_at(sign * (2 * j + 1))], rx1.at[side, j], send.at[S_C],
+                       c1_recv.at[side, j], (dp, z_at(sign))).start()
+            return 0
+        lax.fori_loop(0, high - low + 1, one, 0)
+
+    def reached(side, j, long):
+        remote(terms.at[z], rx1.at[side, j], send.at[S_C], c1_recv.at[side, j],
+               (dp, z_at(1))).wait_recv()
+        total = rx1[side, j].astype(F32)
+        if long:
+            remote(terms.at[z], rx2.at[side, j], send.at[S_C], c2_recv.at[side, j],
+                   (dp, z_at(1))).wait_recv()
+            total = total + rx2[side, j].astype(F32)
+        return total
+
+    def send_on(side, sign, j, long):
+        at = z_at(sign * 2 * j)
+        terms[at] = (terms[at].astype(F32) + reached(side, j, long)).astype(BF16)
+        remote(terms.at[at], rx2.at[side, j - 1], send.at[S_C], c2_recv.at[side, j - 1],
+               (dp, z_at(2 * sign))).start()
+
+    def next_terms(high, low):
+        def one(n, _):
+            for side, sign in sides:
+                send_on(side, sign, high - n, True)
+            return 0
+        lax.fori_loop(0, high - low + 1, one, 0)
+
+    chip = dp // 2
+    core = lax.rem(dp, 2)
+
+    def to_chips(stage, src, dst):
+        def one(n, _):
+            to = lax.rem(dp + 2 * n, N)
+            remote(src, dst, send.at[stage], recv.at[stage], (to, z)).start()
+            return 0
+        lax.fori_loop(1, 16, one, 0)
+
+    def to_sibling(stage, ref):
+        remote(ref, ref, send.at[stage], recv.at[stage], (dp + 1 - 2 * core, z)).start()
+
+    remote(terms.at[z_at(16)], rx2.at[0, 7], send.at[S_C], c2_recv.at[0, 7], (dp, z_at(2))).start()
+    odd_terms(7, 5)
+
     for load in loads[3:8]:
         load.wait()
     gate = jnp.tanh(enc_gate[...])
@@ -154,65 +211,6 @@
 
     to_plane(S_NRM, lambda to: nrm.at[dp], nrm.at[dp])
 
-    for load in loads[8:10]:
-        load.wait()
-    for n in range(4):
-        heads = nt(d_update[...], ow_v[1024 * n : 1024 * (n + 1)]).astype(BF16)
-        for j in range(8):
-            terms[8 * n + j] = heads[:, W * j : W * (j + 1)]
-
-    sides = ((0, 1), (1, -1))
-
-    def first_terms():
-        remote(terms.at[z_at(16)], rx2.at[0, 7], send.at[S_C], c2_recv.at[0, 7],
-               (dp, z_at(2))).start()
-
-        def one(n, _):
-            j = 7 - n
-            for side, sign in sides:
-                remote(terms.at[z_at(sign * (2 * j + 1))], rx1.at[side, j], send.at[S_C],
-                       c1_recv.at[side, j], (dp, z_at(sign))).start()
-            return 0
-        lax.fori_loop(0, 8, one, 0)
-
-    def reached(side, j, long):
-        remote(terms.at[z], rx1.at[side, j], send.at[S_C], c1_recv.at[side, j],
-               (dp, z_at(1))).wait_recv()
-        total = rx1[side, j].astype(F32)
-        if long:
-            remote(terms.at[z], rx2.at[side, j], send.at[S_C], c2_recv.at[side, j],
-                   (dp, z_at(1))).wait_recv()
-            total = total + rx2[side, j].astype(F32)
-        return total
-
-    def send_on(side, sign, j, long):
-        at = z_at(sign * 2 * j)
-        terms[at] = (terms[at].astype(F32) + reached(side, j, long)).astype(BF16)
-        remote(terms.at[at], rx2.at[side, j - 1], send.at[S_C], c2_recv.at[side, j - 1],
-               (dp, z_at(2 * sign))).start()
-
-    def next_terms(high, low):
-        def one(n, _):
-            for side, sign in sides:
-                send_on(side, sign, high - n, True)
-            return 0
-        lax.fori_loop(0, high - low + 1, one, 0)
-
-    chip = dp // 2
-    core = lax.rem(dp, 2)
-
-    def to_chips(stage, src, dst):
-        def one(n, _):
-            to = lax.rem(dp + 2 * n, N)
-            remote(src, dst, send.at[stage], recv.at[stage], (to, z)).start()
-            return 0
-        lax.fori_loop(1, 16, one, 0)
-
-    def to_sibling(stage, ref):
-        remote(ref, ref, send.at[stage], recv.at[stage], (dp + 1 - 2 * core, z)).start()
-
-    first_terms()
-
     for load in loads[10:]:
         load.wait()
     query_pre = nn(text_v[...], qw_v[...])
@@ -223,9 +221,6 @@
     qi_v[...] = jnp.broadcast_to(inv_query, (W, W))
     qs_v[...] = (query_unit * q_gain[...] * scale).astype(BF16)
 
-    send_on(1, -1, 7, False)
-    send_on(0, 1, 7, True)
-    next_terms(6, 6)
 
     @pl.when(owning)
     def _():
@@ -236,19 +231,10 @@
         tile_of(wf, own_tile)[...] = tile
         to_z(S_WAG, lambda to: ws, tile_of(wf, own_tile))
 
-    part = pl.ds(pl.multiple_of(16 * chip, 16), 16)
-    even = lax.rem(z, 2) == core
-
-    @pl.when(even)
-    def _():
-        to_z(
-            S_QT1,
-            lambda to: qw_v.at[pl.ds(pl.multiple_of(256 * to + 16 * chip, 16), 16)],
-            qt.at[core, z // 2, part],
-        )
-        qt[core, z // 2, part] = qw_v[pl.ds(pl.multiple_of(256 * z + 16 * chip, 16), 16)]
-
-    next_terms(5, 3)
+    odd_terms(4, 3)
+    send_on(1, -1, 7, False)
+    send_on(0, 1, 7, True)
+    next_terms(6, 5)
 
     @pl.when(owning)
     def _():
@@ -272,18 +258,20 @@
     own_rows = wf.at[pl.ds(pl.multiple_of(rows0, 32), 32), pl.ds(0, ENC)]
     wg[chip, core] = own_rows[...]
 
+    odd_terms(2, 0)
+    part = pl.ds(pl.multiple_of(16 * chip, 16), 16)
+    even = lax.rem(z, 2) == core
+
     @pl.when(even)
     def _():
-        wait_for(recv.at[S_QT1], kvr.at[pl.ds(0, 15)])
-
-    @pl.when(jnp.logical_not(even))
-    def _():
-        wait_for(recv.at[S_QT1], kvr.at[pl.ds(0, 16)])
-
-    to_chips(S_QT2, qt.at[core, :, part], qt.at[core, :, part])
-
-
-    next_terms(2, 2)
+        to_z(
+            S_QT1,
+            lambda to: qw_v.at[pl.ds(pl.multiple_of(256 * to + 16 * chip, 16), 16)],
+            qt.at[core, z // 2, part],
+        )
+        qt[core, z // 2, part] = qw_v[pl.ds(pl.multiple_of(256 * z + 16 * chip, 16), 16)]
+
+    next_terms(4, 3)
 
     wait_for(recv.at[S_PLA], pr.at[pl.ds(0, N - 1)])
     blocks = jnp.sum(pr[...].reshape(8, 4, 8, W), axis=1)
@@ -298,7 +286,18 @@
     kvr[z] = kvs[z // 8]
     to_chips(S_WG1, wg.at[chip, core], wg.at[chip, core])
 
-    next_terms(1, 1)
+    @pl.when(even)
+    def _():
+        wait_for(recv.at[S_QT1], kvr.at[pl.ds(0, 15)])
+
+    @pl.when(jnp.logical_not(even))
+    def _():
+        wait_for(recv.at[S_QT1], kvr.at[pl.ds(0, 16)])
+
+    to_chips(S_QT2, qt.at[core, :, part], qt.at[core, :, part])
+
+
+    next_terms(2, 1)
 
     row = lax.broadcasted_iota(jnp.int32, (W, 256), 1)
     slot = lax.broadcasted_iota(jnp.int32, (W, 256), 0)
@@ -315,9 +314,6 @@
     d_gate = jnp.tanh(attn_gate[...])
     d_attn = (d_gate * attn_total * valid).astype(BF16)
 
-    wait_for(recv.at[S_QT2], qt.at[0, pl.ds(0, 15)])
-    to_sibling(S_QT3, qt.at[core])
-
     wait_for(recv.at[S_KV], kvr.at[pl.ds(0, N - 1)])
     kv_f = kvr[...].astype(F32)
     keys = kv_f[:, :8].reshape(256, W).astype(BF16)
@@ -343,39 +339,6 @@
     def arrived(from_z):
         remote(dqa.at[from_z], dqa.at[from_z], send.at[S_DQ], dq_recv.at[from_z],
                (dp, z_at(1))).wait_recv()
-
-    for hops in (3, -3, 1, -1):
-        pass_on(z, hops)
-
-    attn_out[...] = (nn(probs_low, values) * valid).astype(BF16)
-    d_scores = d_scores_f.astype(BF16).astype(F32).T.astype(BF16)
-    probs_t = probs_low.astype(F32).T.astype(BF16)
-    d_keys = nn(d_scores, q_scaled)
-    query_part = jnp.sum(d_q_scaled * query_unit, axis=0, keepdims=True) * scale
-    key_part = jnp.sum(
-        d_keys.astype(BF16).astype(F32) * keys.astype(F32), axis=0, keepdims=True
-    ) / k_gain[...]
-    gs[...] = jnp.concatenate([query_part, key_part], axis=0)
-    to_plane(S_G1, lambda to: gs, gr.at[dp])
-    gr[dp] = gs[...]
-
-    d_values = nn(probs_t, d_attn)
-    kgs[...] = jnp.concatenate(
-        [d_keys.reshape(N, 8, W), d_values.reshape(N, 8, W)], axis=1
-    ).astype(BF16)
-    seg = z // 8
-    place = lax.rem(z, 8)
-
-    def to_segment(n, _):
-        to = lax.rem(place + n, 8)
-        remote(kgs.at[pl.ds(4 * to, 4)], kg1.at[place], send.at[S_KG1], recv.at[S_KG1],
-               (dp, 8 * seg + to)).start()
-        return 0
-
-    lax.fori_loop(1, 8, to_segment, 0)
-    kg1[place] = kgs[pl.ds(4 * place, 4)]
-    wait_for(recv.at[S_WG1], wg.at[pl.ds(0, 15), 0])
-    to_sibling(S_WG2, wg.at[:, core])
 
     def text_term(head):
         return nt(dqa[head], qt[lax.rem(head, 2), head // 2])
@@ -413,7 +376,49 @@
             jnp.concatenate([qt[lax.rem(h, 2), h // 2] for h in heads], axis=1),
         )
 
+    for hops in (3, -3, 1, -1):
+        pass_on(z, hops)
+
+    d_scores = d_scores_f.astype(BF16).astype(F32).T.astype(BF16)
+    d_keys = nn(d_scores, q_scaled)
+    query_part = jnp.sum(d_q_scaled * query_unit, axis=0, keepdims=True) * scale
+    key_part = jnp.sum(
+        d_keys.astype(BF16).astype(F32) * keys.astype(F32), axis=0, keepdims=True
+    ) / k_gain[...]
+    gs[...] = jnp.concatenate([query_part, key_part], axis=0)
+    to_plane(S_G1, lambda to: gs, gr.at[dp])
+    gr[dp] = gs[...]
+
     relay(0)
+
+    probs_t = probs_low.astype(F32).T.astype(BF16)
+    d_values = nn(probs_t, d_attn)
+    kgs[...] = jnp.concatenate(
+        [d_keys.reshape(N, 8, W), d_values.reshape(N, 8, W)], axis=1
+    ).astype(BF16)
+    seg = z // 8
+    place = lax.rem(z, 8)
+
+    def to_segment(n, _):
+        to = lax.rem(place + n, 8)
+        remote(kgs.at[pl.ds(4 * to, 4)], kg1.at[place], send.at[S_KG1], recv.at[S_KG1],
+               (dp, 8 * seg + to)).start()
+        return 0
+
+    lax.fori_loop(1, 8, to_segment, 0)
+    kg1[place] = kgs[pl.ds(4 * place, 4)]
+
+    relay(1)
+
+    wait_for(recv.at[S_G1], gr.at[pl.ds(0, N - 1)])
+    gs2[...] = jnp.sum(gr[...], axis=0)
+    to_z(S_G2, lambda to: gs2, gr2.at[z])
+    gr2[z] = gs2[...]
+
+    relay(2)
+
+    wait_for(recv.at[S_QT2], qt.at[0, pl.ds(0, 15)])
+    to_sibling(S_QT3, qt.at[core])
 
     wait_for(recv.at[S_KG1], kg1.at[pl.ds(0, 7)])
     kg2[...] = jnp.sum(kg1[...].astype(F32), axis=0).astype(BF16)
@@ -428,19 +433,16 @@
         def _():
             kgr[seg] = kg2[j]
 
-    wait_for(recv.at[S_G1], gr.at[pl.ds(0, N - 1)])
-    gs2[...] = jnp.sum(gr[...], axis=0)
-    to_z(S_G2, lambda to: gs2, gr2.at[z])
-    gr2[z] = gs2[...]
+    wait_for(recv.at[S_WG1], wg.at[pl.ds(0, 15), 0])
+    to_sibling(S_WG2, wg.at[:, core])
+    attn_out[...] = (nn(probs_low, values) * valid).astype(BF16)
 
     wait_for(recv.at[S_QT3], qt.at[0])
     acc[...] = text_term(z)
-
-    relay(1)
     use(0)
-    relay(2)
+
+    relay(3)
     use(1)
-    relay(3)
     use(2)
     relay(4)
     use(3)
@@ -523,6 +525,19 @@
     @pl.when(even)
     def _():
         wait_for(send.at[S_QT1], kvr.at[pl.ds(0, N - 1)])
+
+
+def hand_over(*refs):
+    sems = refs[15]
+    loads = [pltpu.make_async_copy(refs[n], refs[10 + n], sems.at[n]) for n in range(5)]
+    stores = [pltpu.make_async_copy(refs[10 + n], refs[5 + n], sems.at[5 + n]) for n in range(5)]
+    for load in loads:
+        load.start()
+    for load, store in zip(loads, stores):
+        load.wait()
+        store.start()
+    for store in stores:
+        store.wait()
 
 
 def on_device(
@@ -564,7 +579,7 @@
         pltpu.SemaphoreType.DMA((2, 8)), pltpu.SemaphoreType.DMA((2, 8)),
         pltpu.SemaphoreType.DMA((N,)),
     ]
-    attn, d_text, d_features, d_q_gain, d_k_gain = pl.pallas_call(
+    results = pl.pallas_call(
         kernel,
         out_shape=(
             jax.ShapeDtypeStruct((128, W), BF16),
@@ -581,6 +596,16 @@
         ),
         name="layer",
     )(*arguments)
+    attn, d_text, d_features, d_q_gain, d_k_gain = pl.pallas_call(
+        hand_over,
+        out_shape=tuple(jax.ShapeDtypeStruct(r.shape, r.dtype) for r in results),
+        in_specs=[anywhere] * 5,
+        out_specs=(anywhere,) * 5,
+        scratch_shapes=[pltpu.VMEM(r.shape, r.dtype) for r in results]
+        + [pltpu.SemaphoreType.DMA((10,))],
+        compiler_params=pltpu.CompilerParams(vmem_limit_bytes=60 << 20),
+        name="hand_over",
+    )(*results)
     return attn, d_text, d_features, d_q_gain.reshape(W), d_k_gain.reshape(W)
 
 

time: 148 us -> 140 us (0.946)
  the two profiles are of different devices: /device:TPU:6 before, /device:TPU:16 now
where the time goes in v3:
time: 140 us; the launch traced here: 139 us
  Pallas kernels  137 us (98%)
  between operations  1.94 us (1%)
    pallas_call x1, Pallas kernels, on_device(): pl.pallas_call(kernel, out_shape=(jax.ShapeDtypeStruct((128, W), BF16), j...  136 us

profile of v3, /device:TPU:16, one launch (start us, length us, event | category | flops | bytes accessed | tf_op | source)
XLA Modules:
  0.0 139.4 jit_solution(9201954466440780174)
XLA Ops:
  1.9 135.9 %layer.1 = (bf16[128,128]{1,0:T(8,128)(2,1)}, bf16[128,256]{1,0:T(8,128)(2,1)}, bf16[8,1280]{1,0:T(8,128)(2,1)}, f32[1,128]{1,0:T(1,128)}, f32[1,128]{1,0:T(1,128)}) custom-call(bf16[8,1280]{1,0:T(8,128)(2,1)} %enc_hidden_h.1, bf16[8,1280]{1,0:T(8,128)(2,1)} %enc_branch_h.1, f32[1,1]{1,0:T(1,128)} %bitcast.9.enc_gate_h, f32[10,128]{1,0:T(8,128)} %bitcast.11, ...), custom_call_target="tpu_custom_call" | custom-call | tf_op jit(solution)/shard_map/layer/pallas_call | solution.py:582
  137.8 1.6 %hand_over.1 = (bf16[128,128]{1,0:T(8,128)(2,1)}, bf16[128,256]{1,0:T(8,128)(2,1)}, bf16[8,1280]{1,0:T(8,128)(2,1)}, f32[1,128]{1,0:T(1,128)}, f32[1,128]{1,0:T(1,128)}) custom-call(bf16[128,128]{1,0:T(8,128)(2,1)} %get-tuple-element.15.refs_0_, bf16[128,256]{1,0:T(8,128)(2,1)} %get-tuple-element.16.refs_1_, bf16[8,1280]{1,0:T(8,128)(2,1)} %get-tuple-element.17.refs_2_, ...), custom_call_target="tpu_custom_call" | custom-call | tf_op jit(solution)/shard_map/hand_over/pallas_call | solution.py:599
